TPU v7x, 32 devices: a whole 2x2x4 slice. The times are simulated.
32 devices in a mesh: aux: 2 (over core), occ: 16 (over z, y, x).
Axes of the slice: x: 2, y: 2, z: 4, core: 2. Of those that a mesh axis runs over, the one named last changes fastest.
Arguments:
- factors: float32 [2048, 16, 512], P('aux', 'occ'), may hold values from -0.3 to 0.3
- eps_occ: float32 [16], P('occ'), may hold values from -2 to -0.3
- eps_virt: float32 [512], replicated, may hold values from 0.2 to 3
- pair_mask: int32 [16, 4], P('occ'), may hold values 0 or 1
Outputs:
- gradient: float32 [2048, 16, 512], P('aux', 'occ')
Inputs may be any that keep to these rules, and one draw needn't show every extreme that they name: `pair_mask`: 1 marks a surviving pair.
All inputs are finite; a program needn't handle non-finite values. No bound on the sum of `pair_mask` on one device may be relied on, other than what follows from the above.
Results may differ from a plain program's by a relative error of at most 0.0003.
Values sent between devices are 32-bit elements; how exact they have to be, the bound alone decides.
No kernel may reach another device: no remote copies, remote signals or barrier semaphores. Data moves between devices by JAX's collectives and lax.ppermute only.
A program may use at most 128 MiB of HBM per device.

v0:
```python
import functools

import jax
import jax.numpy as jnp
from jax import lax
from jax.experimental import pallas as pl
from jax.experimental.pallas import tpu as pltpu
from jax.sharding import PartitionSpec as P

LANES = 128
PLANE = 4
CHUNKS = 4
VMEM_LIMIT = 40 * 1024 * 1024
NN = (((1,), (0,)), ((), ()))


def split(value):
    high = value.astype(jnp.bfloat16)
    low = (value - high.astype(jnp.float32)).astype(jnp.bfloat16)
    return high, low


def product(left, right):
    def dot(a, b):
        return lax.dot_general(a, b, NN, preferred_element_type=jnp.float32)

    return dot(left[0], right[0]) + (dot(left[0], right[1]) + dot(left[1], right[0]))


def rows_of(refs, start, count, width):
    lines = width // LANES
    columns = []
    for column in range(lines):
        parts = [ref[pl.ds(start * lines + column, count, stride=lines), :] for ref in refs]
        columns.append(functools.reduce(jnp.add, parts))
    return jnp.concatenate(columns, axis=1)


def call(kernel, inputs, outputs, scratch=(), flops=0, smem=()):
    specs = [pl.BlockSpec(memory_space=pltpu.SMEM)] * len(smem)
    specs += [pl.BlockSpec(memory_space=pltpu.VMEM)] * len(inputs)
    moved = sum(a.size * a.dtype.itemsize for a in (*inputs, *outputs))
    return pl.pallas_call(
        kernel,
        out_shape=outputs,
        in_specs=specs,
        out_specs=[pl.BlockSpec(memory_space=pltpu.VMEM)] * len(outputs),
        scratch_shapes=list(scratch),
        compiler_params=pltpu.CompilerParams(vmem_limit_bytes=VMEM_LIMIT),
        cost_estimate=pl.CostEstimate(flops=flops, bytes_accessed=moved, transcendentals=0),
    )(*smem, *inputs)


def prepare(own, rows, width):
    def kernel(own_ref, high_ref, low_ref, integrals_ref):
        tile = min(256, rows)
        integrals_ref[...] = jnp.zeros_like(integrals_ref)

        def step(at, _):
            start = pl.multiple_of(at * tile, tile)
            block = rows_of([own_ref], start, tile, width)
            turned = split(block.T)
            high_ref[:, pl.ds(start, tile)] = turned[0]
            low_ref[:, pl.ds(start, tile)] = turned[1]
            integrals_ref[...] += product(turned, split(block))
            return 0

        lax.fori_loop(0, rows // tile, step, 0)

    half = jax.ShapeDtypeStruct((width, rows), jnp.bfloat16)
    square = jax.ShapeDtypeStruct((width, width), jnp.float32)
    return call(kernel, [own], [half, half, square], flops=6 * rows * width * width)


def integrate(high, low, slots, first, size, width, before=None):
    count = len(slots)
    chunks = len(slots[0])
    flat = [array for slot in slots for chunk in slot for array in chunk]
    inputs = [high, low] + flat + ([before] if before is not None else [])

    def kernel(*refs):
        high_ref, low_ref = refs[:2]
        given = iter(refs[2 : 2 + len(flat)])
        out_ref = refs[-1]
        for slot in range(count):
            total = None
            for at in range(chunks):
                parts = [next(given) for _ in slots[slot][at]]
                where = pl.ds((first + at) * size, size)
                left = (high_ref[:, where], low_ref[:, where])
                value = product(left, split(rows_of(parts, 0, size, width)))
                total = value if total is None else total + value
            if before is not None:
                total = total + refs[-2][slot]
            out_ref[slot] = total

    out = jax.ShapeDtypeStruct((count, width, width), jnp.float32)
    return call(kernel, inputs, [out], flops=6 * count * chunks * size * width * width)[0]


def contract(partials, slots, signs, row_energy, col_energy, rows, size, width, before=None):
    count = len(slots)
    chunks = len(slots[0])
    lines = width // LANES
    summed = [array for slot in partials for array in slot]
    flat = [array for slot in slots for chunk in slot for array in chunk]
    inputs = [row_energy, col_energy] + summed + flat + ([before] if before is not None else [])

    def kernel(sign_ref, row_ref, col_ref, *refs):
        given = iter(refs)
        sums = [[next(given) for _ in slot] for slot in partials]
        visitors = [[[next(given) for _ in chunk] for chunk in slot] for slot in slots]
        before_ref = next(given) if before is not None else None
        out_ref, high_ref, low_ref = refs[-3:]
        for slot in range(count):
            total = functools.reduce(jnp.add, [ref[...] for ref in sums[slot]])
            energy = row_ref[...] + col_ref[slot : slot + 1, :]
            amplitude = (sign_ref[slot] * total) / energy
            high_ref[slot], low_ref[slot] = split(amplitude.T)
        tile = min(256, size)
        for at in range(chunks):
            for start in range(0, size, tile):
                value = None
                for slot in range(count):
                    block = split(rows_of(visitors[slot][at], start, tile, width))
                    term = product(block, (high_ref[slot], low_ref[slot]))
                    value = term if value is None else value + term
                base = (at * size + start) * lines
                for column in range(lines):
                    lanes = value[:, column * LANES : (column + 1) * LANES]
                    where = pl.ds(base + column, tile, stride=lines)
                    if before_ref is not None:
                        lanes = lanes + before_ref[where, :]
                    out_ref[where, :] = lanes

    out = jax.ShapeDtypeStruct((rows * lines, LANES), jnp.float32)
    held = pltpu.VMEM((count, width, width), jnp.bfloat16)
    flops = 6 * count * rows * width * width
    return call(kernel, inputs, [out], [held, held], flops, [signs])[0]


def on_device(factors, eps_occ, eps_virt, pair_mask):
    rows, occ_rows, virt = factors.shape
    width = occ_rows * virt
    lines = width // LANES
    groups = lax.axis_size("occ")
    shares = lax.axis_size("aux")
    offsets = pair_mask.shape[1]
    size = rows // CHUNKS
    group = lax.axis_index("occ")
    place = group % PLANE

    own = factors.reshape(rows * lines, LANES)
    own_parts = [own[at * size * lines : (at + 1) * size * lines] for at in range(CHUNKS)]

    def swap(block, bit):
        return lax.ppermute(block, "occ", [(g, g ^ bit) for g in range(groups)])

    def up(block):
        return lax.ppermute(block, "occ", [(g, g + PLANE) for g in range(groups - PLANE)])

    def summed(partial):
        if shares == 2:
            return [partial, lax.ppermute(partial, "aux", [(0, 1), (1, 0)])]
        return [lax.psum(partial, "aux")]

    every_eps = lax.all_gather(eps_occ, "occ", tiled=True).reshape(groups, occ_rows)

    def flat_energy(eps_group):
        return (eps_virt[None, :] - eps_group[:, None]).reshape(width)

    row_energy = flat_energy(eps_occ)[:, None]

    def slot_terms(offset):
        source = jnp.maximum(group - offset, 0)
        energy = flat_energy(lax.dynamic_index_in_dim(every_eps, source, 0, keepdims=False))
        flag = lax.dynamic_index_in_dim(pair_mask[0], offset - 1, 0, keepdims=False)
        live = (group >= offset) & (flag > 0)
        return energy, jnp.where(live, -1.0, 0.0).astype(jnp.float32)

    odd_x = place % 2 == 1
    odd_y = place // 2 == 1
    slot_z = slot_terms(PLANE)
    slot_x = slot_terms(jnp.where(odd_x, 1, PLANE - 1))
    slot_y = slot_terms(jnp.int32(PLANE // 2))
    slot_d = slot_terms(jnp.where(odd_x, PLANE - 1, 1))

    from_z, from_x, from_y, from_d = [], [], [], []
    for at in range(CHUNKS):
        from_z.append(up(own_parts[at]))
        from_x.append(swap(jnp.where(odd_x, from_z[at], own_parts[at]), 1))
        from_y.append(swap(jnp.where(odd_y, from_z[at], own_parts[at]), 2))
        from_d.append(swap(from_y[at], 1))

    high, low, own_partial = prepare(own, rows, width)
    own_sum = summed(own_partial)

    def chunks_of(blocks):
        return [[block] for block in blocks]

    def terms(*slots):
        return jnp.stack([s[1] for s in slots]), jnp.stack([s[0] for s in slots])

    partial_z = integrate(high, low, [chunks_of(from_z)], 0, size, width)
    sum_z = [part[0] for part in summed(partial_z)]
    slot_own = (flat_energy(eps_occ), jnp.float32(-1.0))
    signs, col_energy = terms(slot_own, slot_z)
    gradient = contract(
        [own_sum, sum_z], [chunks_of(own_parts), chunks_of(from_z)], signs, row_energy, col_energy, rows, size, width
    )

    last = CHUNKS - 1
    partial = integrate(high, low, [chunks_of(from_x[:last]), chunks_of(from_y[:last])], 0, size, width)
    partial = integrate(high, low, [chunks_of(from_x[last:]), chunks_of(from_y[last:])], last, size, width, partial)
    both = summed(partial)
    signs, col_energy = terms(slot_x, slot_y)
    gradient = contract(
        [[part[slot] for part in both] for slot in range(2)],
        [chunks_of(from_x), chunks_of(from_y)], signs, row_energy, col_energy, rows, size, width, gradient,
    )

    partial = integrate(high, low, [chunks_of(from_d[:last])], 0, size, width)
    partial = integrate(high, low, [chunks_of(from_d[last:])], last, size, width, partial)
    sum_d = [part[0] for part in summed(partial)]
    signs, col_energy = terms(slot_d)
    gradient = contract(
        [sum_d], [chunks_of(from_d)], signs, row_energy, col_energy, rows, size, width, gradient
    )
    return gradient.reshape(rows, occ_rows, virt)


def solution(mesh):
    if mesh.shape["occ"] % PLANE:
        raise ValueError("incomplete plane")
    in_specs = (P("aux", "occ", None), P("occ"), P(), P("occ", None))
    out_specs = P("aux", "occ", None)
    return jax.shard_map(
        on_device, mesh=mesh, in_specs=in_specs, out_specs=out_specs, check_vma=False
    )
```

profile of v0, /device:TPU:0, one launch (start us, length us, event | category | flops | bytes accessed | tf_op | source)
XLA Modules:
  0.0 210.7 jit_solution(10131657036765829280)
XLA Ops:
  0.0 3.0 %fusion = (f32[256,1,512]{2,1,0:T(1,128)S(1)}, f32[256,1,512]{2,1,0:T(1,128)S(1)}, f32[256,1,512]{2,1,0:T(1,128)S(1)}, f32[256,1,512]{2,1,0:T(1,128)S(1)}) fusion(f32[1024,1,512]{2,1,0:T(1,128)} %param.4), kind=kLoop, calls=%fused_computation.23 | loop fusion | bytes 4194304 | tf_op jit(solution)/shard_map/slice | solution.py:154
  3.0 5.0 %collective-permute-start.9 = (f32[1024,128]{1,0:T(8,128)S(1)}, f32[1024,128]{1,0:T(8,128)S(1)}, u32[]{:S(2)}, u32[]{:S(2)}) collective-permute-start(f32[1024,128]{1,0:T(8,128)S(1)} %bitcast.41), channel_id=1, source_target_pairs={{0,4},{1,5},{2,6},{3,7},{4,8},{5,9},{6,10},{7,11},{8,12},{9,13},{1... | collective-permute-start | bytes 1572872 | tf_op jit(solution)/shard_map/ppermute | solution.py:160
  8.0 3.5 %collective-permute-start.3 = (f32[1024,128]{1,0:T(8,128)S(1)}, f32[1024,128]{1,0:T(8,128)S(1)}, u32[]{:S(2)}, u32[]{:S(2)}) collective-permute-start(f32[1024,128]{1,0:T(8,128)S(1)} %bitcast.44), channel_id=1, source_target_pairs={{0,4},{1,5},{2,6},{3,7},{4,8},{5,9},{6,10},{7,11},{8,12},{9,13},{1... | collective-permute-start | bytes 1572872 | tf_op jit(solution)/shard_map/ppermute | solution.py:160
  11.5 4.3 %collective-permute-start = (f32[1024,128]{1,0:T(8,128)S(1)}, f32[1024,128]{1,0:T(8,128)}, u32[]{:S(2)}, u32[]{:S(2)}) collective-permute-start(f32[1024,128]{1,0:T(8,128)S(1)} %bitcast.47), channel_id=1, source_target_pairs={{0,4},{1,5},{2,6},{3,7},{4,8},{5,9},{6,10},{7,11},{8,12},{9,13},{1... | collective-permute-start | bytes 1572872 | tf_op jit(solution)/shard_map/ppermute | solution.py:160
  15.8 2.1 collective-permute-start.6
  17.8 2.4 %collective-permute-done.9.refs_4_.refs_10_ = f32[1024,128]{1,0:T(8,128)S(1)} collective-permute-done((f32[1024,128]{1,0:T(8,128)S(1)}, f32[1024,128]{1,0:T(8,128)S(1)}, u32[]{:S(2)}, u32[]{:S(2)}) %collective-permute-start.9) | collective-permute-done | bytes 524320 | tf_op jit(solution)/shard_map/ppermute | solution.py:160
  21.9 9.6 %collective-permute-done.3.refs_2_.refs_8_ = f32[1024,128]{1,0:T(8,128)S(1)} collective-permute-done((f32[1024,128]{1,0:T(8,128)S(1)}, f32[1024,128]{1,0:T(8,128)S(1)}, u32[]{:S(2)}, u32[]{:S(2)}) %collective-permute-start.3) | collective-permute-done | bytes 524320 | tf_op jit(solution)/shard_map/ppermute | solution.py:160
  33.2 19.6 %collective-permute-done.6.refs_3_.refs_9_ = f32[1024,128]{1,0:T(8,128)} collective-permute-done((f32[1024,128]{1,0:T(8,128)S(1)}, f32[1024,128]{1,0:T(8,128)}, u32[]{:S(2)}, u32[]{:S(2)}) %collective-permute-start.6) | collective-permute-done | bytes 524320 | tf_op jit(solution)/shard_map/ppermute | solution.py:160
  60.8 8.1 %collective-permute-done.15.refs_3_.refs_5_ = f32[1024,128]{1,0:T(8,128)S(1)} collective-permute-done((f32[1024,128]{1,0:T(8,128)S(1)}, f32[1024,128]{1,0:T(8,128)S(1)}, u32[]{:S(2)}, u32[]{:S(2)}) %collective-permute-start.15) | collective-permute-done | bytes 524320 | tf_op jit(solution)/shard_map/ppermute | solution.py:157
  70.4 3.6 %shard_map.46 = (bf16[512,1024]{1,0:T(8,128)(2,1)S(1)}, bf16[512,1024]{1,0:T(8,128)(2,1)S(1)}, f32[512,512]{1,0:T(8,128)}) custom-call(f32[4096,128]{1,0:T(8,128)S(1)} %bitcast.40), custom_call_target="tpu_custom_call" | custom-call | flops 1610612736 | bytes 5242880 | tf_op jit(solution)/shard_map/pallas_call | solution.py:43
  73.9 6.2 %collective-permute-done.16.refs_4_.refs_6_ = f32[1024,128]{1,0:T(8,128)S(1)} collective-permute-done((f32[1024,128]{1,0:T(8,128)S(1)}, f32[1024,128]{1,0:T(8,128)S(1)}, u32[]{:S(2)}, u32[]{:S(2)}) %collective-permute-start.16) | collective-permute-done | bytes 524320 | tf_op jit(solution)/shard_map/ppermute | solution.py:157
  82.1 4.0 %shard_map.49.refs_4_ = f32[2,512,512]{2,1,0:T(8,128)S(1)} custom-call(bf16[512,1024]{1,0:T(8,128)(2,1)S(1)} %get-tuple-element.8.refs_0_, bf16[512,1024]{1,0:T(8,128)(2,1)S(1)} %get-tuple-element.9.refs_1_, f32[1024,128]{1,0:T(8,128)S(1)} %collective-permute-done.14.refs_2_.refs_4_, f32[1024,128]{1,0:T(8,128)S(1)} %collective-permute-done.15.refs_3_.refs_5_, ...), custom_call_target="tpu_custom_call" | custom-call | flops 2415919104 | bytes 7340032 | tf_op jit(solution)/shard_map/pallas_call | solution.py:43
  86.2 4.6 %collective-permute-done.1.refs_3_.refs_11_ = f32[1024,128]{1,0:T(8,128)S(1)} collective-permute-done((f32[1024,128]{1,0:T(8,128)S(1)}, f32[1024,128]{1,0:T(8,128)S(1)}, u32[]{:S(2)}, u32[]{:S(2)}) %collective-permute-start.1) | collective-permute-done | bytes 524320 | tf_op jit(solution)/shard_map/ppermute | solution.py:157
  90.7 2.3 %shard_map.50 = f32[2,512,512]{2,1,0:T(8,128)} custom-call(bf16[512,1024]{1,0:T(8,128)(2,1)S(1)} %get-tuple-element.8.refs_0_, bf16[512,1024]{1,0:T(8,128)(2,1)S(1)} %get-tuple-element.9.refs_1_, f32[1024,128]{1,0:T(8,128)S(1)} %collective-permute-done.13.refs_2_.refs_7_, f32[1024,128]{1,0:T(8,128)S(1)} %collective-permute-done.1.refs_3_.refs_11_, ...), custom_call_target="tpu_custom_call" | custom-call | flops 805306368 | bytes 7340032 | tf_op jit(solution)/shard_map/pallas_call | solution.py:43
  97.1 56.6 %all-reduce = f32[16]{0:T(128)S(1)} all-reduce(f32[16]{0:T(128)S(1)} %dynamic-update-slice), channel_id=1, replica_groups=mesh['aux'=2,'occ'=16] {'occ'}, use_global_device_ids=true, to_apply=%add | all-reduce | flops 16 | bytes 128
  156.5 4.0 %shard_map.51 = f32[1,512,512]{2,1,0:T(8,128)} custom-call(bf16[512,1024]{1,0:T(8,128)(2,1)S(1)} %get-tuple-element.8.refs_0_, bf16[512,1024]{1,0:T(8,128)(2,1)S(1)} %get-tuple-element.9.refs_1_, f32[1024,128]{1,0:T(8,128)S(1)} %copy-done.21, f32[1024,128]{1,0:T(8,128)} %collective-permute-done.6.refs_3_.refs_9_, f32[1024,128]{1,0:T(8,128)S(1)} %copy-done.18, ...), custom_call_target="tpu_custom_call" | custom-call | flops 1610612736 | bytes 5242880 | tf_op jit(solution)/shard_map/pallas_call | solution.py:43
  160.5 2.4 %broadcast_subtract_fusion = (f32[512]{0:T(512)S(1)}, f32[512]{0:T(512)S(1)}, f32[512]{0:T(512)S(1)}, f32[512]{0:T(512)S(1)}, f32[512]{0:T(512)S(1)}) fusion(f32[512]{0:T(512)S(1)} %copy-done.24, f32[]{:T(128)} %bitcast.29, f32[]{:T(128)} %bitcast.18, f32[]{:T(128)} %bitcast.5, f32[]{:T(128)} %bitcast.38, f32[]{:T(128)} %bitcast.20), kind=kLoop, calls=%fused_computation.14 | loop fusion | flops 2560 | bytes 12308 | tf_op jit(solution)/shard_map/sub | solution.py:170
  166.3 2.1 collective-permute-start.2
  168.6 9.5 %collective-permute-done.8.refs_3_ = f32[1024,128]{1,0:T(8,128)} collective-permute-done((f32[1024,128]{1,0:T(8,128)}, f32[1024,128]{1,0:T(8,128)}, u32[]{:S(2)}, u32[]{:S(2)}) %collective-permute-start.8) | collective-permute-done | bytes 524320 | tf_op jit(solution)/shard_map/ppermute | solution.py:157
  178.1 2.8 %shard_map.47.refs_3_ = f32[1,512,512]{2,1,0:T(8,128)S(1)} custom-call(bf16[512,1024]{1,0:T(8,128)(2,1)S(1)} %get-tuple-element.8.refs_0_, bf16[512,1024]{1,0:T(8,128)(2,1)S(1)} %get-tuple-element.9.refs_1_, f32[1024,128]{1,0:T(8,128)} %collective-permute-done.5.refs_2_, f32[1024,128]{1,0:T(8,128)} %collective-permute-done.8.refs_3_, ...), custom_call_target="tpu_custom_call" | custom-call | flops 1207959552 | bytes 4718592 | tf_op jit(solution)/shard_map/pallas_call | solution.py:43
  180.9 8.0 %collective-permute-done.2.refs_2_.refs_5_ = f32[1024,128]{1,0:T(8,128)S(1)} collective-permute-done((f32[1024,128]{1,0:T(8,128)S(1)}, f32[1024,128]{1,0:T(8,128)S(1)}, u32[]{:S(2)}, u32[]{:S(2)}) %collective-permute-start.2) | collective-permute-done | bytes 524320 | tf_op jit(solution)/shard_map/ppermute | solution.py:157
  191.9 6.4 %shard_map.52.refs_12_ = f32[4096,128]{1,0:T(8,128)S(1)} custom-call(f32[2]{0:T(128)S(1)} %pad_maximum_fusion.3.sign_ref, f32[512,1]{1,0:T(8,128)S(1)} %copy.8.row_ref, f32[2,512]{1,0:T(2,128)S(1)} %pad_maximum_fusion.1.col_ref, f32[512,512]{1,0:T(8,128)} %get-tuple-element.10.refs_0_, f32[512,512]{1,0:T(8,128)} %collective-permute-done.18.refs_1_, ...), custom_call_target="tpu_custom_call" | custom-call | flops 3221225472 | bytes 10491904 | tf_op jit(solution)/shard_map/pallas_call | solution.py:43
  200.6 5.2 %shard_map.53.refs_6_ = f32[4096,128]{1,0:T(8,128)S(1)} custom-call(f32[2]{0:T(128)S(1)} %pad_maximum_fusion.2.sign_ref, f32[512,1]{1,0:T(8,128)S(1)} %copy.8.row_ref, f32[2,512]{1,0:T(2,128)S(1)} %pad_maximum_fusion.col_ref, f32[512,512]{1,0:T(8,128)S(1)} %get-tuple-element.14.refs_0_, f32[512,512]{1,0:T(8,128)S(1)} %get-tuple-element.12.refs_1_, ...), custom_call_target="tpu_custom_call" | custom-call | flops 3221225472 | bytes 12589056 | tf_op jit(solution)/shard_map/pallas_call | solution.py:43
  205.8 4.9 %shard_map.54 = f32[4096,128]{1,0:T(8,128)} custom-call(f32[1]{0:T(128)} %bitcast.1.sign_ref, f32[512,1]{1,0:T(8,128)S(1)} %copy.8.row_ref, f32[1,512]{1,0:T(1,128)S(1)} %bitcast.54, f32[512,512]{1,0:T(8,128)S(1)} %bitcast.39, f32[512,512]{1,0:T(8,128)S(1)} %bitcast.53, f32[1024,128]{1,0:T(8,128)} %collective-permute-done.5.refs_2_, ...), custom_call_target="tpu_custom_call" | custom-call | flops 1610612736 | bytes 8392704 | tf_op jit(solution)/shard_map/pallas_call | solution.py:43
  (96 shorter events, 27.0 us)
Async XLA Ops:
  3.0 28.6 %copy-start.1 = (f32[256,1,512]{2,1,0:T(1,128)}, f32[256,1,512]{2,1,0:T(1,128)S(1)}, u32[]{:S(2)}) copy-start(f32[256,1,512]{2,1,0:T(1,128)S(1)} %get-tuple-element.15) | copy-start | bytes 1572868
  3.0 49.8 %copy-start.7 = (f32[256,1,512]{2,1,0:T(1,128)}, f32[256,1,512]{2,1,0:T(1,128)S(1)}, u32[]{:S(2)}) copy-start(f32[256,1,512]{2,1,0:T(1,128)S(1)} %get-tuple-element.18) | copy-start | bytes 1572868
  3.0 55.1 %copy-start.5 = (f32[256,1,512]{2,1,0:T(1,128)}, f32[256,1,512]{2,1,0:T(1,128)S(1)}, u32[]{:S(2)}) copy-start(f32[256,1,512]{2,1,0:T(1,128)S(1)} %get-tuple-element.17) | copy-start | bytes 1572868
  3.0 17.2 %collective-permute-start.9 = (f32[1024,128]{1,0:T(8,128)S(1)}, f32[1024,128]{1,0:T(8,128)S(1)}, u32[]{:S(2)}, u32[]{:S(2)}) collective-permute-start(f32[1024,128]{1,0:T(8,128)S(1)} %bitcast.41), channel_id=1, source_target_pairs={{0,4},{1,5},{2,6},{3,7},{4,8},{5,9},{6,10},{7,11},{8,12},{9,13},{1... | collective-permute-start | bytes 1572872 | tf_op jit(solution)/shard_map/ppermute | solution.py:160
  8.0 23.5 %collective-permute-start.3 = (f32[1024,128]{1,0:T(8,128)S(1)}, f32[1024,128]{1,0:T(8,128)S(1)}, u32[]{:S(2)}, u32[]{:S(2)}) collective-permute-start(f32[1024,128]{1,0:T(8,128)S(1)} %bitcast.44), channel_id=1, source_target_pairs={{0,4},{1,5},{2,6},{3,7},{4,8},{5,9},{6,10},{7,11},{8,12},{9,13},{1... | collective-permute-start | bytes 1572872 | tf_op jit(solution)/shard_map/ppermute | solution.py:160
  11.5 44.6 %collective-permute-start = (f32[1024,128]{1,0:T(8,128)S(1)}, f32[1024,128]{1,0:T(8,128)}, u32[]{:S(2)}, u32[]{:S(2)}) collective-permute-start(f32[1024,128]{1,0:T(8,128)S(1)} %bitcast.47), channel_id=1, source_target_pairs={{0,4},{1,5},{2,6},{3,7},{4,8},{5,9},{6,10},{7,11},{8,12},{9,13},{1... | collective-permute-start | bytes 1572872 | tf_op jit(solution)/shard_map/ppermute | solution.py:160
  15.8 37.1 %collective-permute-start.6 = (f32[1024,128]{1,0:T(8,128)S(1)}, f32[1024,128]{1,0:T(8,128)}, u32[]{:S(2)}, u32[]{:S(2)}) collective-permute-start(f32[1024,128]{1,0:T(8,128)S(1)} %bitcast.50), channel_id=1, source_target_pairs={{0,4},{1,5},{2,6},{3,7},{4,8},{5,9},{6,10},{7,11},{8,12},{9,13},{1... | collective-permute-start | bytes 1572872 | tf_op jit(solution)/shard_map/ppermute | solution.py:160
  20.3 37.2 %collective-permute-start.10 = (f32[1024,128]{1,0:T(8,128)S(1)}, f32[1024,128]{1,0:T(8,128)}, u32[]{:S(2)}, u32[]{:S(2)}) collective-permute-start(f32[1024,128]{1,0:T(8,128)S(1)} %get-tuple-element.20), channel_id=1, source_target_pairs={{0,2},{1,3},{2,0},{3,1},{4,6},{5,7},{6,4},{7,5},{8,10},{9,11},{10,... | collective-permute-start | bytes 1572872 | tf_op jit(solution)/shard_map/ppermute | solution.py:157
  31.6 38.8 %copy-start = (f32[1024,1,512]{2,1,0:T(1,128)S(1)}, f32[1024,1,512]{2,1,0:T(1,128)}, u32[]{:S(2)}) copy-start(f32[1024,1,512]{2,1,0:T(1,128)} %param.4) | copy-start | bytes 6291460
  31.6 27.6 %collective-permute-start.14 = (f32[1024,128]{1,0:T(8,128)S(1)}, f32[1024,128]{1,0:T(8,128)S(1)}, u32[]{:S(2)}, u32[]{:S(2)}) collective-permute-start(f32[1024,128]{1,0:T(8,128)S(1)} %get-tuple-element.23), channel_id=1, source_target_pairs={{0,1},{1,0},{2,3},{3,2},{4,5},{5,4},{6,7},{7,6},{8,9},{9,8},{10,11... | collective-permute-start | bytes 1572872 | tf_op jit(solution)/shard_map/ppermute | solution.py:157
  53.9 14.9 %collective-permute-start.15 = (f32[1024,128]{1,0:T(8,128)S(1)}, f32[1024,128]{1,0:T(8,128)S(1)}, u32[]{:S(2)}, u32[]{:S(2)}) collective-permute-start(f32[1024,128]{1,0:T(8,128)S(1)} %get-tuple-element.21), channel_id=1, source_target_pairs={{0,1},{1,0},{2,3},{3,2},{4,5},{5,4},{6,7},{7,6},{8,9},{9,8},{10,11... | collective-permute-start | bytes 1572872 | tf_op jit(solution)/shard_map/ppermute | solution.py:157
  55.5 24.6 %collective-permute-start.16 = (f32[1024,128]{1,0:T(8,128)S(1)}, f32[1024,128]{1,0:T(8,128)S(1)}, u32[]{:S(2)}, u32[]{:S(2)}) collective-permute-start(f32[1024,128]{1,0:T(8,128)S(1)} %get-tuple-element.19), channel_id=1, source_target_pairs={{0,1},{1,0},{2,3},{3,2},{4,5},{5,4},{6,7},{7,6},{8,9},{9,8},{10,11... | collective-permute-start | bytes 1572872 | tf_op jit(solution)/shard_map/ppermute | solution.py:157
  56.0 24.1 %collective-permute-start.4 = (f32[1024,128]{1,0:T(8,128)S(1)}, f32[1024,128]{1,0:T(8,128)}, u32[]{:S(2)}, u32[]{:S(2)}) collective-permute-start(f32[1024,128]{1,0:T(8,128)S(1)} %get-tuple-element.24), channel_id=1, source_target_pairs={{0,2},{1,3},{2,0},{3,1},{4,6},{5,7},{6,4},{7,5},{8,10},{9,11},{10,... | collective-permute-start | bytes 1572872 | tf_op jit(solution)/shard_map/ppermute | solution.py:157
  57.5 24.6 %collective-permute-start.7 = (f32[1024,128]{1,0:T(8,128)S(1)}, f32[1024,128]{1,0:T(8,128)S(1)}, u32[]{:S(2)}, u32[]{:S(2)}) collective-permute-start(f32[1024,128]{1,0:T(8,128)S(1)} %get-tuple-element.22), channel_id=1, source_target_pairs={{0,2},{1,3},{2,0},{3,1},{4,6},{5,7},{6,4},{7,5},{8,10},{9,11},{10,... | collective-permute-start | bytes 1572872 | tf_op jit(solution)/shard_map/ppermute | solution.py:157
  59.2 31.5 %collective-permute-start.1 = (f32[1024,128]{1,0:T(8,128)S(1)}, f32[1024,128]{1,0:T(8,128)S(1)}, u32[]{:S(2)}, u32[]{:S(2)}) collective-permute-start(f32[1024,128]{1,0:T(8,128)S(1)} %get-tuple-element.26), channel_id=1, source_target_pairs={{0,2},{1,3},{2,0},{3,1},{4,6},{5,7},{6,4},{7,5},{8,10},{9,11},{10,... | collective-permute-start | bytes 1572872 | tf_op jit(solution)/shard_map/ppermute | solution.py:157
  68.9 21.9 %collective-permute-start.13 = (f32[1024,128]{1,0:T(8,128)S(1)}, f32[1024,128]{1,0:T(8,128)S(1)}, u32[]{:S(2)}, u32[]{:S(2)}) collective-permute-start(f32[1024,128]{1,0:T(8,128)S(1)} %get-tuple-element.25), channel_id=1, source_target_pairs={{0,1},{1,0},{2,3},{3,2},{4,5},{5,4},{6,7},{7,6},{8,9},{9,8},{10,11... | collective-permute-start | bytes 1572872 | tf_op jit(solution)/shard_map/ppermute | solution.py:157
  93.1 105.4 %collective-permute-start.17 = (f32[2,512,512]{2,1,0:T(8,128)}, f32[2,512,512]{2,1,0:T(8,128)}, u32[]{:S(2)}, u32[]{:S(2)}) collective-permute-start(f32[2,512,512]{2,1,0:T(8,128)} %shard_map.50), channel_id=1, source_target_pairs={{0,16},{16,0},{1,17},{17,1},{2,18},{18,2},{3,19},{19,3},{4,20},{20... | collective-permute-start | bytes 6291464 | tf_op jit(solution)/shard_map/ppermute | solution.py:164
  93.1 69.9 %collective-permute-start.11 = (f32[1024,128]{1,0:T(8,128)}, f32[1024,128]{1,0:T(8,128)}, u32[]{:S(2)}, u32[]{:S(2)}) collective-permute-start(f32[1024,128]{1,0:T(8,128)} %collective-permute-done.10.refs_7_.refs_10_), channel_id=1, source_target_pairs={{0,1},{1,0},{2,3},{3,2},{4,5},{5,4},{6,7},{7,6},{8,9},{9,8},{10,11... | collective-permute-start | bytes 1572872 | tf_op jit(solution)/shard_map/ppermute | solution.py:157
  94.6 71.8 %collective-permute-start.5 = (f32[1024,128]{1,0:T(8,128)}, f32[1024,128]{1,0:T(8,128)}, u32[]{:S(2)}, u32[]{:S(2)}) collective-permute-start(f32[1024,128]{1,0:T(8,128)} %collective-permute-done.4.refs_5_.refs_8_), channel_id=1, source_target_pairs={{0,1},{1,0},{2,3},{3,2},{4,5},{5,4},{6,7},{7,6},{8,9},{9,8},{10,11... | collective-permute-start | bytes 1572872 | tf_op jit(solution)/shard_map/ppermute | solution.py:157
  95.1 96.4 %collective-permute-start.18 = (f32[512,512]{1,0:T(8,128)}, f32[512,512]{1,0:T(8,128)}, u32[]{:S(2)}, u32[]{:S(2)}) collective-permute-start(f32[512,512]{1,0:T(8,128)} %get-tuple-element.10.refs_0_), channel_id=1, source_target_pairs={{0,16},{16,0},{1,17},{17,1},{2,18},{18,2},{3,19},{19,3},{4,20},{20... | collective-permute-start | bytes 3145736 | tf_op jit(solution)/shard_map/ppermute | solution.py:164
  160.5 31.0 %collective-permute-start.19 = (f32[1,512,512]{2,1,0:T(8,128)}, f32[1,512,512]{2,1,0:T(8,128)}, u32[]{:S(2)}, u32[]{:S(2)}) collective-permute-start(f32[1,512,512]{2,1,0:T(8,128)} %shard_map.51), channel_id=1, source_target_pairs={{0,16},{16,0},{1,17},{17,1},{2,18},{18,2},{3,19},{19,3},{4,20},{20... | collective-permute-start | bytes 3145736 | tf_op jit(solution)/shard_map/ppermute | solution.py:164
  163.0 15.1 %collective-permute-start.8 = (f32[1024,128]{1,0:T(8,128)}, f32[1024,128]{1,0:T(8,128)}, u32[]{:S(2)}, u32[]{:S(2)}) collective-permute-start(f32[1024,128]{1,0:T(8,128)} %copy-done.15), channel_id=1, source_target_pairs={{0,1},{1,0},{2,3},{3,2},{4,5},{5,4},{6,7},{7,6},{8,9},{9,8},{10,11... | collective-permute-start | bytes 1572872 | tf_op jit(solution)/shard_map/ppermute | solution.py:157
  166.3 22.5 %collective-permute-start.2 = (f32[1024,128]{1,0:T(8,128)S(1)}, f32[1024,128]{1,0:T(8,128)S(1)}, u32[]{:S(2)}, u32[]{:S(2)}) collective-permute-start(f32[1024,128]{1,0:T(8,128)S(1)} %collective-permute-done.1.refs_3_.refs_11_), channel_id=1, source_target_pairs={{0,1},{1,0},{2,3},{3,2},{4,5},{5,4},{6,7},{7,6},{8,9},{9,8},{10,11... | collective-permute-start | bytes 1572872 | tf_op jit(solution)/shard_map/ppermute | solution.py:157
  189.5 16.2 %collective-permute-start.12 = (f32[1,512,512]{2,1,0:T(8,128)S(1)}, f32[1,512,512]{2,1,0:T(8,128)S(1)}, u32[]{:S(2)}, u32[]{:S(2)}) collective-permute-start(f32[1,512,512]{2,1,0:T(8,128)S(1)} %shard_map.48), channel_id=1, source_target_pairs={{0,16},{16,0},{1,17},{17,1},{2,18},{18,2},{3,19},{19,3},{4,20},{20... | collective-permute-start | bytes 3145736 | tf_op jit(solution)/shard_map/ppermute | solution.py:164
  (22 other events, 151.9 us)
where the time goes:
time: 211 us
  waiting for transfers between devices  70 us (33%)
  blocking collectives  56.6 us (27%)
  Pallas kernels  33.8 us (16%)
  starting transfers between devices  29.4 us (14%)
  local copies, waits for them, and re-layouts  12.3 us (6%)
  other arithmetic  4.88 us (2%)
  between operations  3.64 us (2%)
    unnamed x1, blocking collectives  56.6 us
    ppermute x12, waiting for transfers between devices, swap(): return lax.ppermute(block, 'occ', [(g, g ^ bit) for g in range(groups)])  38.4 us
    pallas_call x9, Pallas kernels, call(): pl.pallas_call(kernel, out_shape=outputs, in_specs=specs, out_specs=[pl.B...  33.8 us
    ppermute x4, waiting for transfers between devices, up(): lax.ppermute(block, 'occ', [(g, g + PLANE) for g in range(groups - PLANE)])  31.6 us
    ppermute x4, starting transfers between devices, up(): lax.ppermute(block, 'occ', [(g, g + PLANE) for g in range(groups - PLANE)])  14.8 us
    ppermute x12, starting transfers between devices, swap(): return lax.ppermute(block, 'occ', [(g, g ^ bit) for g in range(groups)])  14.5 us
  transfers between devices with their start and end apart: 20, of which 9 were waited for; matrix products, arithmetic and copies ran while one was open for 5% of the time, Pallas kernels for 13%

commit v1 on v0

v1 whole, which is shorter than its diff:
```python
import functools

import jax
import jax.numpy as jnp
from jax import lax
from jax.experimental import pallas as pl
from jax.experimental.pallas import tpu as pltpu
from jax.sharding import PartitionSpec as P

LANES = 128
SUBLANES = 8
PLANE = 4
CHUNKS = 4
VMEM_LIMIT = 40 * 1024 * 1024
NN = (((1,), (0,)), ((), ()))


def split(value):
    high = value.astype(jnp.bfloat16)
    low = (value - high.astype(jnp.float32)).astype(jnp.bfloat16)
    return high, low


def product(left, right):
    def dot(a, b):
        return lax.dot_general(a, b, NN, preferred_element_type=jnp.float32)

    return dot(left[0], right[0]) + (dot(left[0], right[1]) + dot(left[1], right[0]))


def rows_of(ref, base, start, count, width):
    lines = width // LANES
    first = base + start * lines
    columns = [ref[pl.ds(first + at, count, stride=lines), :] for at in range(lines)]
    return jnp.concatenate(columns, axis=1)


def distinct(slots):
    return list({id(array): array for slot in slots for array, _ in slot}.values())


def call(kernel, inputs, outputs, scratch=(), flops=0, smem=()):
    specs = [pl.BlockSpec(memory_space=pltpu.SMEM)] * len(smem)
    specs += [pl.BlockSpec(memory_space=pltpu.VMEM)] * len(inputs)
    moved = sum(a.size * a.dtype.itemsize for a in (*inputs, *outputs))
    return pl.pallas_call(
        kernel,
        out_shape=outputs,
        in_specs=specs,
        out_specs=[pl.BlockSpec(memory_space=pltpu.VMEM)] * len(outputs),
        scratch_shapes=list(scratch),
        compiler_params=pltpu.CompilerParams(vmem_limit_bytes=VMEM_LIMIT),
        cost_estimate=pl.CostEstimate(flops=flops, bytes_accessed=moved, transcendentals=0),
    )(*smem, *inputs)


def prepare(own, rows, width):
    def kernel(own_ref, high_ref, low_ref, integrals_ref):
        tile = min(256, rows)
        integrals_ref[...] = jnp.zeros_like(integrals_ref)

        def step(at, _):
            start = pl.multiple_of(at * tile, tile)
            block = rows_of(own_ref, 0, start, tile, width)
            turned = split(block.T)
            high_ref[:, pl.ds(start, tile)] = turned[0]
            low_ref[:, pl.ds(start, tile)] = turned[1]
            integrals_ref[...] += product(turned, split(block))
            return 0

        lax.fori_loop(0, rows // tile, step, 0)

    half = jax.ShapeDtypeStruct((width, rows), jnp.bfloat16)
    square = jax.ShapeDtypeStruct((width, width), jnp.float32)
    return call(kernel, [own], [half, half, square], flops=6 * rows * width * width)


def integrate(turned, slots, first, size, width, before=()):
    count = len(slots)
    flat = distinct(slots)
    before = list(before)

    def kernel(high_ref, low_ref, *refs):
        ref_of = {id(array): ref for array, ref in zip(flat, refs)}
        before_refs = refs[len(flat) : len(flat) + len(before)]
        outs = refs[len(flat) + len(before) :]
        for slot in range(count):
            total = before_refs[slot][...] if before else None
            for number, (array, base) in enumerate(slots[slot], first[slot]):
                where = pl.ds(number * size, size)
                left = (high_ref[:, where], low_ref[:, where])
                value = product(left, split(rows_of(ref_of[id(array)], base, 0, size, width)))
                total = value if total is None else total + value
            outs[slot][...] = total

    out = [jax.ShapeDtypeStruct((width, width), jnp.float32)] * count
    flops = 6 * sum(map(len, slots)) * size * width * width
    return call(kernel, [*turned, *flat, *before], out, flops=flops)


def contract(partials, slots, signs, eps_own, eps_virt, size, before=None):
    count = len(slots)
    chunks = len(slots[0])
    virt = eps_virt.shape[1]
    occ_rows = eps_own.shape[0]
    width = occ_rows * virt
    lines = width // LANES
    summed = [array for slot in partials for array in slot]
    flat = distinct(slots)
    inputs = [eps_virt] + summed + flat + ([before] if before is not None else [])

    def kernel(sign_ref, own_ref, virt_ref, *refs):
        given = iter(refs)
        sums = [[next(given) for _ in slot] for slot in partials]
        ref_of = {id(array): next(given) for array in flat}
        before_ref = next(given) if before is not None else None
        out_ref, high_ref, low_ref = refs[-3:]
        virtual = virt_ref[...]
        row = jnp.concatenate([virtual - own_ref[i] for i in range(occ_rows)], axis=1)
        row = jnp.broadcast_to(row, (SUBLANES, width)).T[:, :1]
        for slot in range(count):
            total = functools.reduce(jnp.add, [ref[...] for ref in sums[slot]])
            array, base = slots[slot][0]
            at = base + size * lines
            line = ref_of[id(array)][at : at + 1, :]
            column = jnp.concatenate([virtual - line[:, j : j + 1] for j in range(occ_rows)], axis=1)
            amplitude = (sign_ref[slot] * total) / (row + column)
            high_ref[slot], low_ref[slot] = split(amplitude.T)
        tile = min(256, size)
        for at in range(chunks):
            for start in range(0, size, tile):
                value = None
                for slot in range(count):
                    array, base = slots[slot][at]
                    block = split(rows_of(ref_of[id(array)], base, start, tile, width))
                    term = product(block, (high_ref[slot], low_ref[slot]))
                    value = term if value is None else value + term
                base = (at * size + start) * lines
                for column in range(lines):
                    lanes = value[:, column * LANES : (column + 1) * LANES]
                    where = pl.ds(base + column, tile, stride=lines)
                    if before_ref is not None:
                        lanes = lanes + before_ref[where, :]
                    out_ref[where, :] = lanes

    rows = chunks * size
    out = jax.ShapeDtypeStruct((rows * lines, LANES), jnp.float32)
    held = pltpu.VMEM((count, width, width), jnp.bfloat16)
    flops = 6 * count * rows * width * width
    return call(kernel, inputs, [out], [held, held], flops, [signs, eps_own])[0]


def after(block, *others):
    return lax.optimization_barrier((block, *others))[0]


def on_device(factors, eps_occ, eps_virt, pair_mask):
    rows, occ_rows, virt = factors.shape
    width = occ_rows * virt
    lines = width // LANES
    groups = lax.axis_size("occ")
    shares = lax.axis_size("aux")
    size = rows // CHUNKS
    last = CHUNKS - 1
    group = lax.axis_index("occ")
    place = group % PLANE
    odd_x = place % 2 == 1
    odd_y = place // 2 == 1

    own = factors.reshape(rows * lines, LANES)
    energies = jnp.zeros((SUBLANES * LANES,), jnp.float32).at[:occ_rows].set(eps_occ)
    energies = energies.reshape(SUBLANES, LANES)

    def part(whole, at):
        block = whole[at * size * lines : (at + 1) * size * lines]
        return jnp.concatenate([block, energies]) if at == 0 else block

    def swap(block, bit):
        return lax.ppermute(block, "occ", [(g, g ^ bit) for g in range(groups)])

    def up(block):
        return lax.ppermute(block, "occ", [(g, g + PLANE) for g in range(groups - PLANE)])

    def totals(partial):
        if shares == 2:
            return [partial, lax.ppermute(partial, "aux", [(0, 1), (1, 0)])]
        return [lax.psum(partial, "aux")]

    def sign(offset):
        flag = lax.dynamic_index_in_dim(pair_mask[0], offset - 1, 0, keepdims=False)
        return jnp.where((group >= offset) & (flag > 0), -1.0, 0.0).astype(jnp.float32)

    sign_own = jnp.float32(-1.0)
    sign_z = sign(jnp.int32(PLANE))
    sign_x = sign(jnp.where(odd_x, 1, PLANE - 1))
    sign_y = sign(jnp.int32(PLANE // 2))
    sign_d = sign(jnp.where(odd_x, PLANE - 1, 1))

    def add(partials, slots, signs, before=None):
        return contract(partials, slots, jnp.stack(signs), eps_occ, eps_virt[None, :], size, before)

    from_z, from_x, from_y, from_d = [], [], [], []
    from_z.append(up(part(own, 0)))
    high, low, partial_own = prepare(own, rows, width)
    turned = (high, low)
    sums_own = totals(partial_own)
    ready = [partial_own]
    for at in range(CHUNKS):
        send_x = after(jnp.where(odd_x, from_z[at], part(own, at)), *ready)
        send_y = jnp.where(odd_y, from_z[at], part(own, at))
        from_x.append(swap(send_x, 1))
        from_y.append(swap(send_y, 2))
        if at < last:
            from_z.append(up(part(after(own, from_z[at]), at + 1)))
        ready = [from_x[at]]
        from_d.append(swap(after(from_y[at], from_d[at - 1] if at else from_x[0]), 1))

    cut = size * lines
    slot_own = [(part(own, 0), 0)] + [(own, at * cut) for at in range(1, CHUNKS)]
    slot_z, slot_x, slot_y, slot_d = (
        [(block, 0) for block in blocks] for blocks in (from_z, from_x, from_y, from_d)
    )

    (partial_z,) = integrate(turned, [slot_z], [0], size, width)
    gradient = add([sums_own, totals(partial_z)], [slot_own, slot_z], [sign_own, sign_z])
    turned = after(turned, gradient)
    early = integrate(
        turned, [slot_x[:last], slot_y[:last], slot_d[: last - 1]], [0, 0, 0], size, width
    )
    partial_x, partial_y, partial_d = integrate(
        turned, [slot_x[last:], slot_y[last:], slot_d[last - 1 : last]], [last, last, last - 1], size, width, early
    )
    (partial_d,) = integrate(turned, [slot_d[last:]], [last], size, width, [partial_d])
    gradient = add(
        [totals(partial_x), totals(partial_y), totals(partial_d)],
        [slot_x, slot_y, slot_d], [sign_x, sign_y, sign_d], gradient,
    )
    return gradient.reshape(rows, occ_rows, virt)


def solution(mesh):
    if mesh.shape["occ"] % PLANE:
        raise ValueError("incomplete plane")
    in_specs = (P("aux", "occ", None), P("occ"), P(), P("occ", None))
    out_specs = P("aux", "occ", None)
    return jax.shard_map(
        on_device, mesh=mesh, in_specs=in_specs, out_specs=out_specs, check_vma=False
    )
```

time: 211 us -> 150 us (0.71)
  blocking collectives: 56.6 us -> 0 us
  waiting for transfers between devices: 70 us -> 51 us
  local copies, waits for them, and re-layouts: 12.3 us -> 20.2 us
  starting transfers between devices: 29.4 us -> 36.9 us
    unnamed x1 -> x0, blocking collectives: 56.6 us -> none
    unnamed x55 -> x78, local copies, waits for them, and re-layouts: 4.16 us -> 15.3 us
    ppermute x12, waiting for transfers between devices: 38.4 us -> 28 us  [swap(): return lax.ppermute(block, 'occ', [(g, g ^ bit) for g in range(groups)])]
    ppermute x4, waiting for transfers between devices: 31.6 us -> 21.2 us  [up(): lax.ppermute(block, 'occ', [(g, g + PLANE) for g in range(groups - PLANE)])]
    ppermute x4, starting transfers between devices: 14.8 us -> 19.2 us  [up(): lax.ppermute(block, 'occ', [(g, g + PLANE) for g in range(groups - PLANE)])]
    squeeze x2 -> x0, local copies, waits for them, and re-layouts: 3.72 us -> none  [on_device(): part[slot]]
    ppermute x12, starting transfers between devices: 14.5 us -> 17.1 us  [swap(): return lax.ppermute(block, 'occ', [(g, g ^ bit) for g in range(groups)])]
    sub x1 -> x0, other arithmetic: 2.35 us -> none  [flat_energy(): return (eps_virt[None, :] - eps_group[:, None]).reshape(width)]
  transfers between devices with their start and end apart: 20 -> 21, of which waited for: 9 -> 12; matrix products, arithmetic and copies ran while one was open for 5% -> 3% of each run, Pallas kernels for 13% -> 15%
where the time goes in v1:
time: 150 us; the launch traced here: 149 us
  waiting for transfers between devices  51 us (34%)
  starting transfers between devices  36.9 us (25%)
  Pallas kernels  33.6 us (22%)
  local copies, waits for them, and re-layouts  20.2 us (13%)
  other arithmetic  4.1 us (3%)
  between operations  3.53 us (2%)
    pallas_call x7, Pallas kernels, call(): pl.pallas_call(kernel, out_shape=outputs, in_specs=specs, out_specs=[pl.B...  33.6 us
    ppermute x12, waiting for transfers between devices, swap(): return lax.ppermute(block, 'occ', [(g, g ^ bit) for g in range(groups)])  28 us
    ppermute x4, waiting for transfers between devices, up(): lax.ppermute(block, 'occ', [(g, g + PLANE) for g in range(groups - PLANE)])  21.2 us
    ppermute x4, starting transfers between devices, up(): lax.ppermute(block, 'occ', [(g, g + PLANE) for g in range(groups - PLANE)])  19.2 us
    ppermute x12, starting transfers between devices, swap(): return lax.ppermute(block, 'occ', [(g, g ^ bit) for g in range(groups)])  17.1 us
    unnamed x78, local copies, waits for them, and re-layouts  15.3 us
    slice x4, local copies, waits for them, and re-layouts, part(): block = whole[at * size * lines:(at + 1) * size * lines]  4.19 us
    select_n x4, other arithmetic, on_device(): send_y = jnp.where(odd_y, from_z[at], part(own, at))  3.13 us
  transfers between devices with their start and end apart: 21, of which 12 were waited for; matrix products, arithmetic and copies ran while one was open for 3% of the time, Pallas kernels for 15%

profile of v1, /device:TPU:0, one launch (start us, length us, event | category | flops | bytes accessed | tf_op | source)
XLA Modules:
  0.0 149.3 jit_solution(12787375385579046109)
XLA Ops:
  0.7 4.1 %fusion = (f32[256,1,512]{2,1,0:T(1,128)}, f32[256,1,512]{2,1,0:T(1,128)}, f32[256,1,512]{2,1,0:T(1,128)S(1)}, f32[256,1,512]{2,1,0:T(1,128)}) fusion(f32[1024,1,512]{2,1,0:T(1,128)} %param.6), kind=kLoop, calls=%fused_computation.14 | loop fusion | bytes 4194304 | tf_op jit(solution)/shard_map/slice | solution.py:175
  6.4 5.8 %collective-permute-start.1 = (f32[1032,128]{1,0:T(8,128)}, f32[1032,128]{1,0:T(8,128)}, u32[]{:S(2)}, u32[]{:S(2)}) collective-permute-start(f32[1032,128]{1,0:T(8,128)} %pad_maximum_fusion.refs_4_), channel_id=1, source_target_pairs={{0,4},{1,5},{2,6},{3,7},{4,8},{5,9},{6,10},{7,11},{8,12},{9,13},{1... | collective-permute-start | bytes 1585160 | tf_op jit(solution)/shard_map/ppermute | solution.py:182
  12.2 3.6 %shard_map.46 = (bf16[512,1024]{1,0:T(8,128)(2,1)S(1)}, bf16[512,1024]{1,0:T(8,128)(2,1)S(1)}, f32[512,512]{1,0:T(8,128)}) custom-call(f32[4096,128]{1,0:T(8,128)S(1)} %bitcast.17), custom_call_target="tpu_custom_call" | custom-call | flops 1610612736 | bytes 5242880 | tf_op jit(solution)/shard_map/pallas_call | solution.py:46
  15.8 7.1 %collective-permute-done.1.refs_0_.refs_6_ = f32[1032,128]{1,0:T(8,128)} collective-permute-done((f32[1032,128]{1,0:T(8,128)}, f32[1032,128]{1,0:T(8,128)}, u32[]{:S(2)}, u32[]{:S(2)}) %collective-permute-start.1) | collective-permute-done | bytes 528416 | tf_op jit(solution)/shard_map/ppermute | solution.py:182
  23.0 4.4 %collective-permute-start.2 = (f32[1024,128]{1,0:T(8,128)S(1)}, f32[1024,128]{1,0:T(8,128)S(1)}, u32[]{:S(2)}, u32[]{:S(2)}) collective-permute-start(f32[1024,128]{1,0:T(8,128)S(1)} %slice.54), channel_id=1, source_target_pairs={{0,4},{1,5},{2,6},{3,7},{4,8},{5,9},{6,10},{7,11},{8,12},{9,13},{1... | collective-permute-start | bytes 1572872 | tf_op jit(solution)/shard_map/ppermute | solution.py:182
  28.5 1.6 %collective-permute-start.6 = (f32[1032,128]{1,0:T(8,128)S(1)}, f32[1032,128]{1,0:T(8,128)S(1)}, u32[]{:S(2)}, u32[]{:S(2)}) collective-permute-start(f32[1032,128]{1,0:T(8,128)S(1)} %get-tuple-element.47), channel_id=1, source_target_pairs={{0,1},{1,0},{2,3},{3,2},{4,5},{5,4},{6,7},{7,6},{8,9},{9,8},{10,11... | collective-permute-start | bytes 1585160 | tf_op jit(solution)/shard_map/ppermute | solution.py:179
  31.6 6.1 %collective-permute-done.2.refs_1_.refs_7_ = f32[1024,128]{1,0:T(8,128)S(1)} collective-permute-done((f32[1024,128]{1,0:T(8,128)S(1)}, f32[1024,128]{1,0:T(8,128)S(1)}, u32[]{:S(2)}, u32[]{:S(2)}) %collective-permute-start.2) | collective-permute-done | bytes 524320 | tf_op jit(solution)/shard_map/ppermute | solution.py:182
  37.7 4.4 %collective-permute-start.3 = (f32[1024,128]{1,0:T(8,128)S(1)}, f32[1024,128]{1,0:T(8,128)S(1)}, u32[]{:S(2)}, u32[]{:S(2)}) collective-permute-start(f32[1024,128]{1,0:T(8,128)S(1)} %slice.55), channel_id=1, source_target_pairs={{0,4},{1,5},{2,6},{3,7},{4,8},{5,9},{6,10},{7,11},{8,12},{9,13},{1... | collective-permute-start | bytes 1572872 | tf_op jit(solution)/shard_map/ppermute | solution.py:182
  43.8 1.6 %collective-permute-start.12 = (f32[1024,128]{1,0:T(8,128)S(1)}, f32[1024,128]{1,0:T(8,128)S(1)}, u32[]{:S(2)}, u32[]{:S(2)}) collective-permute-start(f32[1024,128]{1,0:T(8,128)S(1)} %get-tuple-element.67), channel_id=1, source_target_pairs={{0,2},{1,3},{2,0},{3,1},{4,6},{5,7},{6,4},{7,5},{8,10},{9,11},{10,... | collective-permute-start | bytes 1572872 | tf_op jit(solution)/shard_map/ppermute | solution.py:179
  45.4 6.1 %collective-permute-done.3.refs_2_.refs_8_ = f32[1024,128]{1,0:T(8,128)S(1)} collective-permute-done((f32[1024,128]{1,0:T(8,128)S(1)}, f32[1024,128]{1,0:T(8,128)S(1)}, u32[]{:S(2)}, u32[]{:S(2)}) %collective-permute-start.3) | collective-permute-done | bytes 524320 | tf_op jit(solution)/shard_map/ppermute | solution.py:182
  51.5 4.6 %collective-permute-start.4 = (f32[1024,128]{1,0:T(8,128)S(1)}, f32[1024,128]{1,0:T(8,128)S(1)}, u32[]{:S(2)}, u32[]{:S(2)}) collective-permute-start(f32[1024,128]{1,0:T(8,128)S(1)} %slice.56), channel_id=1, source_target_pairs={{0,4},{1,5},{2,6},{3,7},{4,8},{5,9},{6,10},{7,11},{8,12},{9,13},{1... | collective-permute-start | bytes 1572872 | tf_op jit(solution)/shard_map/ppermute | solution.py:182
  56.2 1.6 %collective-permute-start.7 = (f32[1024,128]{1,0:T(8,128)S(1)}, f32[1024,128]{1,0:T(8,128)S(1)}, u32[]{:S(2)}, u32[]{:S(2)}) collective-permute-start(f32[1024,128]{1,0:T(8,128)S(1)} %get-tuple-element.48), channel_id=1, source_target_pairs={{0,1},{1,0},{2,3},{3,2},{4,5},{5,4},{6,7},{7,6},{8,9},{9,8},{10,11... | collective-permute-start | bytes 1572872 | tf_op jit(solution)/shard_map/ppermute | solution.py:179
  58.7 1.6 %collective-permute-start.11 = (f32[1024,128]{1,0:T(8,128)S(1)}, f32[1024,128]{1,0:T(8,128)}, u32[]{:S(2)}, u32[]{:S(2)}) collective-permute-start(f32[1024,128]{1,0:T(8,128)S(1)} %get-tuple-element.69), channel_id=1, source_target_pairs={{0,2},{1,3},{2,0},{3,1},{4,6},{5,7},{6,4},{7,5},{8,10},{9,11},{10,... | collective-permute-start | bytes 1572872 | tf_op jit(solution)/shard_map/ppermute | solution.py:179
  62.4 2.0 %collective-permute-done.4.refs_3_.refs_9_ = f32[1024,128]{1,0:T(8,128)S(1)} collective-permute-done((f32[1024,128]{1,0:T(8,128)S(1)}, f32[1024,128]{1,0:T(8,128)S(1)}, u32[]{:S(2)}, u32[]{:S(2)}) %collective-permute-start.4) | collective-permute-done | bytes 524320 | tf_op jit(solution)/shard_map/ppermute | solution.py:182
  64.4 4.0 %shard_map.47.refs_2_ = f32[512,512]{1,0:T(8,128)} custom-call(bf16[512,1024]{1,0:T(8,128)(2,1)S(1)} %get-tuple-element.45.high_ref, bf16[512,1024]{1,0:T(8,128)(2,1)S(1)} %get-tuple-element.46.low_ref, f32[1032,128]{1,0:T(8,128)} %collective-permute-done.1.refs_0_.refs_6_, f32[1024,128]{1,0:T(8,128)S(1)} %collective-permute-done.2.refs_1_.refs_7_, ...), custom_call_target="tpu_custom_call" | custom-call | flops 1610612736 | bytes 5246976 | tf_op jit(solution)/shard_map/pallas_call | solution.py:46
  68.4 2.6 %collective-permute-done.7.refs_1_.refs_7_ = f32[1024,128]{1,0:T(8,128)S(1)} collective-permute-done((f32[1024,128]{1,0:T(8,128)S(1)}, f32[1024,128]{1,0:T(8,128)S(1)}, u32[]{:S(2)}, u32[]{:S(2)}) %collective-permute-start.7) | collective-permute-done | bytes 524320 | tf_op jit(solution)/shard_map/ppermute | solution.py:179
  73.5 1.5 %collective-permute-start.10 = (f32[1024,128]{1,0:T(8,128)}, f32[1024,128]{1,0:T(8,128)}, u32[]{:S(2)}, u32[]{:S(2)}) collective-permute-start(f32[1024,128]{1,0:T(8,128)} %get-tuple-element.71), channel_id=1, source_target_pairs={{0,2},{1,3},{2,0},{3,1},{4,6},{5,7},{6,4},{7,5},{8,10},{9,11},{10,... | collective-permute-start | bytes 1572872 | tf_op jit(solution)/shard_map/ppermute | solution.py:179
  75.0 7.2 %collective-permute-done.15.refs_7_.refs_15_ = f32[1024,128]{1,0:T(8,128)S(1)} collective-permute-done((f32[1024,128]{1,0:T(8,128)S(1)}, f32[1024,128]{1,0:T(8,128)S(1)}, u32[]{:S(2)}, u32[]{:S(2)}) %collective-permute-start.15) | collective-permute-done | bytes 524320 | tf_op jit(solution)/shard_map/ppermute | solution.py:179
  85.9 7.6 %collective-permute-done.8.refs_2_.refs_8_ = f32[1024,128]{1,0:T(8,128)} collective-permute-done((f32[1024,128]{1,0:T(8,128)}, f32[1024,128]{1,0:T(8,128)}, u32[]{:S(2)}, u32[]{:S(2)}) %collective-permute-start.8) | collective-permute-done | bytes 524320 | tf_op jit(solution)/shard_map/ppermute | solution.py:179
  95.0 9.7 %collective-permute-done.16.refs_2_.refs_16_ = f32[1024,128]{1,0:T(8,128)} collective-permute-done((f32[1024,128]{1,0:T(8,128)}, f32[1024,128]{1,0:T(8,128)}, u32[]{:S(2)}, u32[]{:S(2)}) %collective-permute-start.16) | collective-permute-done | bytes 524320 | tf_op jit(solution)/shard_map/ppermute | solution.py:179
  109.5 6.6 %shard_map.48.refs_18_ = f32[4096,128]{1,0:T(8,128)S(1)} custom-call(f32[2]{0:T(128)S(1)} %pad_maximum_fusion.2.sign_ref, f32[1]{0:T(128)S(6)} %copy.6.own_ref, f32[1,512]{1,0:T(1,128)S(1)} %bitcast.22, f32[512,512]{1,0:T(8,128)} %get-tuple-element.41.refs_0_, f32[512,512]{1,0:T(8,128)} %collective-permute-done.refs_1_, f32[512,512]{1,0:T(8,128)} %shard_map.47.refs_2_, ...), custom_call_target="tpu_custom_call" | custom-call | flops 3221225472 | bytes 11020288 | tf_op jit(solution)/shard_map/pallas_call | solution.py:46
  117.5 4.6 %shard_map.49 = (f32[512,512]{1,0:T(8,128)S(1)}, f32[512,512]{1,0:T(8,128)S(1)}, f32[512,512]{1,0:T(8,128)S(1)}) custom-call(bf16[512,1024]{1,0:T(8,128)(2,1)S(1)} %get-tuple-element.45.high_ref, bf16[512,1024]{1,0:T(8,128)(2,1)S(1)} %copy-done.2, f32[1032,128]{1,0:T(8,128)S(1)} %copy-done.14, f32[1024,128]{1,0:T(8,128)S(1)} %copy-done.26, ...), custom_call_target="tpu_custom_call" | custom-call | flops 3221225472 | bytes 9449472 | tf_op jit(solution)/shard_map/pallas_call | solution.py:46
  122.2 3.4 %shard_map.50 = (f32[512,512]{1,0:T(8,128)}, f32[512,512]{1,0:T(8,128)}, f32[512,512]{1,0:T(8,128)S(1)}) custom-call(bf16[512,1024]{1,0:T(8,128)(2,1)S(1)} %get-tuple-element.45.high_ref, bf16[512,1024]{1,0:T(8,128)(2,1)S(1)} %copy-done.2, f32[1024,128]{1,0:T(8,128)S(1)} %collective-permute-done.9.refs_0_.refs_9_, ...), custom_call_target="tpu_custom_call" | custom-call | flops 1207959552 | bytes 9961472 | tf_op jit(solution)/shard_map/pallas_call | solution.py:46
  138.5 10.8 %shard_map.52 = f32[4096,128]{1,0:T(8,128)} custom-call(f32[3]{0:T(128)S(1)} %pad_maximum_fusion.1.sign_ref, f32[1]{0:T(128)S(6)} %copy.6.own_ref, f32[1,512]{1,0:T(1,128)S(1)} %bitcast.23, f32[512,512]{1,0:T(8,128)} %get-tuple-element.57.refs_0_, f32[512,512]{1,0:T(8,128)} %collective-permute-done.17.refs_1_, f32[512,512]{1,0:T(8,128)} %get-tuple-element.58.refs_2_, ...), custom_call_target="tpu_custom_call" | custom-call | flops 4831838208 | bytes 16791552 | tf_op jit(solution)/shard_map/pallas_call | solution.py:46
  (116 shorter events, 33.3 us)
Async XLA Ops:
  6.4 16.5 %collective-permute-start.1 = (f32[1032,128]{1,0:T(8,128)}, f32[1032,128]{1,0:T(8,128)}, u32[]{:S(2)}, u32[]{:S(2)}) collective-permute-start(f32[1032,128]{1,0:T(8,128)} %pad_maximum_fusion.refs_4_), channel_id=1, source_target_pairs={{0,4},{1,5},{2,6},{3,7},{4,8},{5,9},{6,10},{7,11},{8,12},{9,13},{1... | collective-permute-start | bytes 1585160 | tf_op jit(solution)/shard_map/ppermute | solution.py:182
  15.8 48.6 %copy-start.1 = (bf16[512,1024]{1,0:T(8,128)(2,1)}, bf16[512,1024]{1,0:T(8,128)(2,1)S(1)}, u32[]{:S(2)}) copy-start(bf16[512,1024]{1,0:T(8,128)(2,1)S(1)} %get-tuple-element.46.low_ref) | copy-start | bytes 3145732
  15.8 27.9 %copy-start.37 = (f32[256,1,512]{2,1,0:T(1,128)S(1)}, f32[256,1,512]{2,1,0:T(1,128)}, u32[]{:S(2)}) copy-start(f32[256,1,512]{2,1,0:T(1,128)} %get-tuple-element.61) | copy-start | bytes 1572868
  23.0 14.7 %collective-permute-start.2 = (f32[1024,128]{1,0:T(8,128)S(1)}, f32[1024,128]{1,0:T(8,128)S(1)}, u32[]{:S(2)}, u32[]{:S(2)}) collective-permute-start(f32[1024,128]{1,0:T(8,128)S(1)} %slice.54), channel_id=1, source_target_pairs={{0,4},{1,5},{2,6},{3,7},{4,8},{5,9},{6,10},{7,11},{8,12},{9,13},{1... | collective-permute-start | bytes 1572872 | tf_op jit(solution)/shard_map/ppermute | solution.py:182
  28.5 13.6 %collective-permute-start.6 = (f32[1032,128]{1,0:T(8,128)S(1)}, f32[1032,128]{1,0:T(8,128)S(1)}, u32[]{:S(2)}, u32[]{:S(2)}) collective-permute-start(f32[1032,128]{1,0:T(8,128)S(1)} %get-tuple-element.47), channel_id=1, source_target_pairs={{0,1},{1,0},{2,3},{3,2},{4,5},{5,4},{6,7},{7,6},{8,9},{9,8},{10,11... | collective-permute-start | bytes 1585160 | tf_op jit(solution)/shard_map/ppermute | solution.py:179
  30.1 12.3 %collective-permute-start.13 = (f32[1032,128]{1,0:T(8,128)S(1)}, f32[1032,128]{1,0:T(8,128)S(1)}, u32[]{:S(2)}, u32[]{:S(2)}) collective-permute-start(f32[1032,128]{1,0:T(8,128)S(1)} %get-tuple-element.65), channel_id=1, source_target_pairs={{0,2},{1,3},{2,0},{3,1},{4,6},{5,7},{6,4},{7,5},{8,10},{9,11},{10,... | collective-permute-start | bytes 1585160 | tf_op jit(solution)/shard_map/ppermute | solution.py:179
  37.7 13.8 %collective-permute-start.3 = (f32[1024,128]{1,0:T(8,128)S(1)}, f32[1024,128]{1,0:T(8,128)S(1)}, u32[]{:S(2)}, u32[]{:S(2)}) collective-permute-start(f32[1024,128]{1,0:T(8,128)S(1)} %slice.55), channel_id=1, source_target_pairs={{0,4},{1,5},{2,6},{3,7},{4,8},{5,9},{6,10},{7,11},{8,12},{9,13},{1... | collective-permute-start | bytes 1572872 | tf_op jit(solution)/shard_map/ppermute | solution.py:182
  42.4 17.8 %collective-permute-start.14 = (f32[1032,128]{1,0:T(8,128)S(1)}, f32[1032,128]{1,0:T(8,128)S(1)}, u32[]{:S(2)}, u32[]{:S(2)}) collective-permute-start(f32[1032,128]{1,0:T(8,128)S(1)} %collective-permute-done.13.refs_3_.refs_10_), channel_id=1, source_target_pairs={{0,1},{1,0},{2,3},{3,2},{4,5},{5,4},{6,7},{7,6},{8,9},{9,8},{10,11... | collective-permute-start | bytes 1585160 | tf_op jit(solution)/shard_map/ppermute | solution.py:179
  43.8 14.9 %collective-permute-start.12 = (f32[1024,128]{1,0:T(8,128)S(1)}, f32[1024,128]{1,0:T(8,128)S(1)}, u32[]{:S(2)}, u32[]{:S(2)}) collective-permute-start(f32[1024,128]{1,0:T(8,128)S(1)} %get-tuple-element.67), channel_id=1, source_target_pairs={{0,2},{1,3},{2,0},{3,1},{4,6},{5,7},{6,4},{7,5},{8,10},{9,11},{10,... | collective-permute-start | bytes 1572872 | tf_op jit(solution)/shard_map/ppermute | solution.py:179
  51.5 12.8 %collective-permute-start.4 = (f32[1024,128]{1,0:T(8,128)S(1)}, f32[1024,128]{1,0:T(8,128)S(1)}, u32[]{:S(2)}, u32[]{:S(2)}) collective-permute-start(f32[1024,128]{1,0:T(8,128)S(1)} %slice.56), channel_id=1, source_target_pairs={{0,4},{1,5},{2,6},{3,7},{4,8},{5,9},{6,10},{7,11},{8,12},{9,13},{1... | collective-permute-start | bytes 1572872 | tf_op jit(solution)/shard_map/ppermute | solution.py:182
  56.1 50.2 %collective-permute-start = (f32[512,512]{1,0:T(8,128)}, f32[512,512]{1,0:T(8,128)}, u32[]{:S(2)}, u32[]{:S(2)}) collective-permute-start(f32[512,512]{1,0:T(8,128)} %get-tuple-element.41.refs_0_), channel_id=1, source_target_pairs={{0,16},{16,0},{1,17},{17,1},{2,18},{18,2},{3,19},{19,3},{4,20},{20... | collective-permute-start | bytes 3145736 | tf_op jit(solution)/shard_map/ppermute | solution.py:186
  56.2 14.8 %collective-permute-start.7 = (f32[1024,128]{1,0:T(8,128)S(1)}, f32[1024,128]{1,0:T(8,128)S(1)}, u32[]{:S(2)}, u32[]{:S(2)}) collective-permute-start(f32[1024,128]{1,0:T(8,128)S(1)} %get-tuple-element.48), channel_id=1, source_target_pairs={{0,1},{1,0},{2,3},{3,2},{4,5},{5,4},{6,7},{7,6},{8,9},{9,8},{10,11... | collective-permute-start | bytes 1572872 | tf_op jit(solution)/shard_map/ppermute | solution.py:179
  58.7 14.9 %collective-permute-start.11 = (f32[1024,128]{1,0:T(8,128)S(1)}, f32[1024,128]{1,0:T(8,128)}, u32[]{:S(2)}, u32[]{:S(2)}) collective-permute-start(f32[1024,128]{1,0:T(8,128)S(1)} %get-tuple-element.69), channel_id=1, source_target_pairs={{0,2},{1,3},{2,0},{3,1},{4,6},{5,7},{6,4},{7,5},{8,10},{9,11},{10,... | collective-permute-start | bytes 1572872 | tf_op jit(solution)/shard_map/ppermute | solution.py:179
  61.1 21.2 %collective-permute-start.15 = (f32[1024,128]{1,0:T(8,128)S(1)}, f32[1024,128]{1,0:T(8,128)S(1)}, u32[]{:S(2)}, u32[]{:S(2)}) collective-permute-start(f32[1024,128]{1,0:T(8,128)S(1)} %collective-permute-done.12.refs_4_.refs_11_), channel_id=1, source_target_pairs={{0,1},{1,0},{2,3},{3,2},{4,5},{5,4},{6,7},{7,6},{8,9},{9,8},{10,11... | collective-permute-start | bytes 1572872 | tf_op jit(solution)/shard_map/ppermute | solution.py:179
  68.4 37.9 %copy-start.31 = (f32[512]{0:T(512)S(1)}, f32[512]{0:T(512)}, u32[]{:S(2)}) copy-start(f32[512]{0:T(512)} %param.8) | copy-start | bytes 6148
  68.4 37.9 %collective-permute-start.5 = (f32[512,512]{1,0:T(8,128)}, f32[512,512]{1,0:T(8,128)}, u32[]{:S(2)}, u32[]{:S(2)}) collective-permute-start(f32[512,512]{1,0:T(8,128)} %shard_map.47.refs_2_), channel_id=1, source_target_pairs={{0,16},{16,0},{1,17},{17,1},{2,18},{18,2},{3,19},{19,3},{4,20},{20... | collective-permute-start | bytes 3145736 | tf_op jit(solution)/shard_map/ppermute | solution.py:186
  71.0 22.6 %collective-permute-start.8 = (f32[1024,128]{1,0:T(8,128)}, f32[1024,128]{1,0:T(8,128)}, u32[]{:S(2)}, u32[]{:S(2)}) collective-permute-start(f32[1024,128]{1,0:T(8,128)} %get-tuple-element.49), channel_id=1, source_target_pairs={{0,1},{1,0},{2,3},{3,2},{4,5},{5,4},{6,7},{7,6},{8,9},{9,8},{10,11... | collective-permute-start | bytes 1572872 | tf_op jit(solution)/shard_map/ppermute | solution.py:179
  73.5 21.5 %collective-permute-start.10 = (f32[1024,128]{1,0:T(8,128)}, f32[1024,128]{1,0:T(8,128)}, u32[]{:S(2)}, u32[]{:S(2)}) collective-permute-start(f32[1024,128]{1,0:T(8,128)} %get-tuple-element.71), channel_id=1, source_target_pairs={{0,2},{1,3},{2,0},{3,1},{4,6},{5,7},{6,4},{7,5},{8,10},{9,11},{10,... | collective-permute-start | bytes 1572872 | tf_op jit(solution)/shard_map/ppermute | solution.py:179
  83.0 21.8 %collective-permute-start.16 = (f32[1024,128]{1,0:T(8,128)}, f32[1024,128]{1,0:T(8,128)}, u32[]{:S(2)}, u32[]{:S(2)}) collective-permute-start(f32[1024,128]{1,0:T(8,128)} %collective-permute-done.11.refs_5_.refs_12_), channel_id=1, source_target_pairs={{0,1},{1,0},{2,3},{3,2},{4,5},{5,4},{6,7},{7,6},{8,9},{9,8},{10,11... | collective-permute-start | bytes 1572872 | tf_op jit(solution)/shard_map/ppermute | solution.py:179
  93.5 28.6 %collective-permute-start.9 = (f32[1024,128]{1,0:T(8,128)}, f32[1024,128]{1,0:T(8,128)S(1)}, u32[]{:S(2)}, u32[]{:S(2)}) collective-permute-start(f32[1024,128]{1,0:T(8,128)} %get-tuple-element.50), channel_id=1, source_target_pairs={{0,1},{1,0},{2,3},{3,2},{4,5},{5,4},{6,7},{7,6},{8,9},{9,8},{10,11... | collective-permute-start | bytes 1572872 | tf_op jit(solution)/shard_map/ppermute | solution.py:179
  104.8 21.9 %collective-permute-start.19 = (f32[1024,128]{1,0:T(8,128)}, f32[1024,128]{1,0:T(8,128)S(1)}, u32[]{:S(2)}, u32[]{:S(2)}) collective-permute-start(f32[1024,128]{1,0:T(8,128)} %collective-permute-done.10.refs_1_.refs_13_), channel_id=1, source_target_pairs={{0,1},{1,0},{2,3},{3,2},{4,5},{5,4},{6,7},{7,6},{8,9},{9,8},{10,11... | collective-permute-start | bytes 1572872 | tf_op jit(solution)/shard_map/ppermute | solution.py:179
  125.6 3.9 %collective-permute-start.17 = (f32[512,512]{1,0:T(8,128)}, f32[512,512]{1,0:T(8,128)}, u32[]{:S(2)}, u32[]{:S(2)}) collective-permute-start(f32[512,512]{1,0:T(8,128)} %get-tuple-element.57.refs_0_), channel_id=1, source_target_pairs={{0,16},{16,0},{1,17},{17,1},{2,18},{18,2},{3,19},{19,3},{4,20},{20... | collective-permute-start | bytes 3145736 | tf_op jit(solution)/shard_map/ppermute | solution.py:186
  125.6 4.5 %collective-permute-start.18 = (f32[512,512]{1,0:T(8,128)}, f32[512,512]{1,0:T(8,128)}, u32[]{:S(2)}, u32[]{:S(2)}) collective-permute-start(f32[512,512]{1,0:T(8,128)} %get-tuple-element.58.refs_2_), channel_id=1, source_target_pairs={{0,16},{16,0},{1,17},{17,1},{2,18},{18,2},{3,19},{19,3},{4,20},{20... | collective-permute-start | bytes 3145736 | tf_op jit(solution)/shard_map/ppermute | solution.py:186
  127.5 3.7 %collective-permute-start.20 = (f32[512,512]{1,0:T(8,128)S(1)}, f32[512,512]{1,0:T(8,128)S(1)}, u32[]{:S(2)}, u32[]{:S(2)}) collective-permute-start(f32[512,512]{1,0:T(8,128)S(1)} %shard_map.51.refs_4_), channel_id=1, source_target_pairs={{0,16},{16,0},{1,17},{17,1},{2,18},{18,2},{3,19},{19,3},{4,20},{20... | collective-permute-start | bytes 3145736 | tf_op jit(solution)/shard_map/ppermute | solution.py:186
  (36 other events, 254.4 us)

commit v2 on v1

v2 whole, which is shorter than its diff:
```python
import functools

import jax
import jax.numpy as jnp
from jax import lax
from jax.experimental import pallas as pl
from jax.experimental.pallas import tpu as pltpu
from jax.sharding import PartitionSpec as P

LANES = 128
SUBLANES = 8
PLANE = 4
CHUNKS = 4
VMEM_LIMIT = 16 * 1024 * 1024
NN = (((1,), (0,)), ((), ()))


def split(value):
    high = value.astype(jnp.bfloat16)
    low = (value - high.astype(jnp.float32)).astype(jnp.bfloat16)
    return high, low


def deep_left(value):
    high, low = split(value)
    return jnp.concatenate([high, low, high], axis=1)


def deep_right(value):
    high, low = split(value)
    return jnp.concatenate([high, high, low], axis=0)


def dot(left, right):
    return lax.dot_general(left, right, NN, preferred_element_type=jnp.float32)


def rows_of(places, start, count, width):
    lines = width // LANES
    columns = []
    for at in range(lines):
        parts = [ref[pl.ds(base + start * lines + at, count, stride=lines), :] for ref, base in places]
        columns.append(functools.reduce(jnp.add, parts))
    return jnp.concatenate(columns, axis=1)


def distinct(slots):
    return list({id(array): array for slot in slots for chunk in slot for array, _ in chunk}.values())


def located(chunk, ref_of):
    return [(ref_of[id(array)], base) for array, base in chunk]


def call(kernel, inputs, outputs, scratch=(), flops=0, smem=()):
    specs = [pl.BlockSpec(memory_space=pltpu.SMEM)] * len(smem)
    specs += [pl.BlockSpec(memory_space=pltpu.VMEM)] * len(inputs)
    moved = sum(a.size * a.dtype.itemsize for a in (*inputs, *outputs))
    return pl.pallas_call(
        kernel,
        out_shape=outputs,
        in_specs=specs,
        out_specs=[pl.BlockSpec(memory_space=pltpu.VMEM)] * len(outputs),
        scratch_shapes=list(scratch),
        compiler_params=pltpu.CompilerParams(vmem_limit_bytes=VMEM_LIMIT),
        cost_estimate=pl.CostEstimate(flops=flops, bytes_accessed=moved, transcendentals=0),
    )(*smem, *inputs)


def prepare(own, rows, width):
    def kernel(own_ref, high_ref, low_ref, integrals_ref):
        tile = min(256, rows)
        integrals_ref[...] = jnp.zeros_like(integrals_ref)

        def step(at, _):
            start = pl.multiple_of(at * tile, tile)
            block = rows_of([(own_ref, 0)], start, tile, width)
            high, low = split(block.T)
            high_ref[:, pl.ds(start, tile)] = high
            low_ref[:, pl.ds(start, tile)] = low
            left = jnp.concatenate([high, low, high], axis=1)
            integrals_ref[...] += dot(left, deep_right(block))
            return 0

        lax.fori_loop(0, rows // tile, step, 0)

    half = jax.ShapeDtypeStruct((width, rows), jnp.bfloat16)
    square = jax.ShapeDtypeStruct((width, width), jnp.float32)
    return call(kernel, [own], [half, half, square], flops=6 * rows * width * width)


def integrate(turned, slots, first, size, width, before=()):
    count = len(slots)
    flat = distinct(slots)
    before = list(before)

    def kernel(high_ref, low_ref, *refs):
        ref_of = {id(array): ref for array, ref in zip(flat, refs)}
        before_refs = refs[len(flat) : len(flat) + len(before)]
        outs = refs[len(flat) + len(before) :]
        for slot in range(count):
            left, right = [], []
            for number, chunk in enumerate(slots[slot], first[slot]):
                where = pl.ds(number * size, size)
                high, low = high_ref[:, where], low_ref[:, where]
                left.append(jnp.concatenate([high, low, high], axis=1))
                right.append(deep_right(rows_of(located(chunk, ref_of), 0, size, width)))
            total = dot(jnp.concatenate(left, axis=1), jnp.concatenate(right, axis=0))
            outs[slot][...] = total + before_refs[slot][...] if before else total

    out = [jax.ShapeDtypeStruct((width, width), jnp.float32)] * count
    flops = 6 * sum(map(len, slots)) * size * width * width
    return call(kernel, [*turned, *flat, *before], out, flops=flops)


def contract(partials, slots, signs, energies, eps_virt, size, before=None):
    count = len(slots)
    chunks = len(slots[0])
    virt = eps_virt.shape[1]
    occ_rows = energies[0].shape[0]
    width = occ_rows * virt
    lines = width // LANES
    summed = [array for slot in partials for array in slot]
    flat = distinct(slots)
    inputs = [eps_virt] + summed + flat + ([before] if before is not None else [])

    def kernel(sign_ref, *refs):
        energy_refs, virt_ref, refs = refs[: count + 1], refs[count + 1], refs[count + 2 :]
        given = iter(refs)
        sums = [[next(given) for _ in slot] for slot in partials]
        ref_of = {id(array): next(given) for array in flat}
        before_ref = next(given) if before is not None else None
        out_ref, right_ref = refs[-2:]

        def line(ref):
            virtual = virt_ref[...]
            return jnp.concatenate([virtual - ref[i] for i in range(occ_rows)], axis=1)

        row = jnp.broadcast_to(line(energy_refs[0]), (SUBLANES, width)).T[:, :1]
        for slot in range(count):
            total = functools.reduce(jnp.add, [ref[...] for ref in sums[slot]])
            amplitude = (sign_ref[slot] * total) / (row + line(energy_refs[slot + 1]))
            right_ref[pl.ds(slot * 3 * width, 3 * width), :] = deep_right(amplitude.T)
        tile = min(256, size)
        for at in range(chunks):
            for start in range(0, size, tile):
                left = []
                for slot in range(count):
                    left.append(deep_left(rows_of(located(slots[slot][at], ref_of), start, tile, width)))
                value = dot(jnp.concatenate(left, axis=1), right_ref[...])
                base = (at * size + start) * lines
                for column in range(lines):
                    lanes = value[:, column * LANES : (column + 1) * LANES]
                    where = pl.ds(base + column, tile, stride=lines)
                    if before_ref is not None:
                        lanes = lanes + before_ref[where, :]
                    out_ref[where, :] = lanes

    rows = chunks * size
    out = jax.ShapeDtypeStruct((rows * lines, LANES), jnp.float32)
    held = pltpu.VMEM((count * 3 * width, width), jnp.bfloat16)
    flops = 6 * count * rows * width * width
    return call(kernel, inputs, [out], [held], flops, [signs, *energies])[0]


def after(block, *others):
    return lax.optimization_barrier((block, *others))[0]


def on_device(factors, eps_occ, eps_virt, pair_mask):
    rows, occ_rows, virt = factors.shape
    width = occ_rows * virt
    lines = width // LANES
    groups = lax.axis_size("occ")
    shares = lax.axis_size("aux")
    size = rows // CHUNKS
    cut = size * lines
    half = CHUNKS // 2
    group = lax.axis_index("occ")
    place = group % PLANE
    odd_x = place % 2 == 1

    own = factors.reshape(rows * lines, LANES)

    def shifted(block, offset):
        return lax.ppermute(block, "occ", [(g, g + offset) for g in range(groups - offset)])

    def within(block, moves, first_plane=0):
        planes = range(first_plane * PLANE, groups, PLANE)
        return lax.ppermute(block, "occ", [(g + a, g + b) for g in planes for a, b in moves])

    def totals(partial):
        if shares == 2:
            return [partial, lax.ppermute(partial, "aux", [(0, 1), (1, 0)])]
        return [lax.psum(partial, "aux")]

    def sign(offset):
        flag = lax.dynamic_index_in_dim(pair_mask[0], offset - 1, 0, keepdims=False)
        return jnp.where((group >= offset) & (flag > 0), -1.0, 0.0).astype(jnp.float32)

    def add(partials, slots, signs, energies, before=None):
        return contract(partials, slots, jnp.stack(signs), [eps_occ, *energies], eps_virt[None, :], size, before)

    parts = [slice(0, half * cut), slice(half * cut, CHUNKS * cut)]
    from_z = [shifted(own[:cut], PLANE)]
    eps_of = [shifted(eps_occ, offset) for offset in range(1, PLANE + 1)]
    own_d = within(own[parts[0]], [(1, 2)])
    own_x = [within(own[parts[0]], [(0, 1), (2, 3)])]
    own_y = [within(own[parts[0]], [(0, 2), (1, 3)])]
    high, low, partial_own = prepare(own, rows, width)
    turned = (high, low)
    sums_own = totals(partial_own)

    from_x, from_y = [], []
    for at in range(CHUNKS):
        from_x.append(within(from_z[at], [(1, 0), (3, 2)], 1))
        from_y.append(within(from_z[at], [(2, 0), (3, 1)], 1))
        if at == 0:
            mine = after(own, from_z[0], partial_own, *eps_of)
        if at == 1:
            mine = after(own, from_z[1], from_y[0], own_d, own_x[0], own_y[0])
            own_x.append(within(mine[parts[1]], [(0, 1), (2, 3)]))
            own_y.append(within(mine[parts[1]], [(0, 2), (1, 3)]))
        if at == 2:
            mine = after(own, from_z[2], from_y[1], from_x[0])
        if at + 1 < CHUNKS:
            from_z.append(shifted(mine[(at + 1) * cut : (at + 2) * cut], PLANE))
    own_d_x = within(own_x[0], [(1, 3)])
    own_d_y = within(own_y[1], [(2, 3), (3, 2)])
    from_d = []
    for at in range(CHUNKS):
        sent = after(from_y[at], *(from_d[at - 1] if 0 < at <= half else []))
        if at < half:
            from_d.append([within(sent, [(0, 1), (1, 0)], 1)])
        else:
            from_d.append([within(sent, [(0, 1)], 1), within(from_x[at], [(2, 0)], 1)])

    def half_of(pieces, at):
        return pieces[at // half], (at % half) * cut

    slot_own = [[(own, at * cut)] for at in range(CHUNKS)]
    slot_z = [[(from_z[at], 0)] for at in range(CHUNKS)]
    slot_x = [[half_of(own_x, at), (from_x[at], 0)] for at in range(CHUNKS)]
    slot_y = [[half_of(own_y, at), (from_y[at], 0)] for at in range(CHUNKS)]
    slot_d = [[(own_d, at * cut), (own_d_x, at * cut), (from_d[at][0], 0)] for at in range(half)]
    slot_d += [
        [(own_d_y, (at - half) * cut), (from_d[at][0], 0), (from_d[at][1], 0)] for at in range(half, CHUNKS)
    ]

    def chosen(offset):
        return jnp.where(odd_x, eps_of[offset], eps_of[PLANE - 2 - offset])

    offset_x = jnp.where(odd_x, 1, PLANE - 1)
    offset_d = PLANE - offset_x

    last = CHUNKS - 1
    (partial_z,) = integrate(after(turned, own_x[1], own_y[1], from_x[1], from_y[2]), [slot_z], [0], size, width)
    gradient = add(
        [after(sums_own, *from_d[0], from_x[2]), totals(partial_z)], [slot_own, slot_z],
        [jnp.float32(-1.0), sign(jnp.int32(PLANE))], [eps_occ, eps_of[PLANE - 1]],
    )
    early = integrate(after(turned, gradient), [slot_x[:last], slot_y[:last]], [0, 0], size, width)
    partial_x, partial_y = integrate(
        after(turned, own_d_x, own_d_y, *from_d[1], *from_d[2]), [slot_x[last:], slot_y[last:]], [last, last], size, width, early
    )
    gradient = add(
        [totals(partial_x), totals(partial_y)], [slot_x, slot_y],
        [sign(offset_x), sign(jnp.int32(PLANE // 2))], [chosen(0), eps_of[PLANE // 2 - 1]], gradient,
    )
    partial_d = integrate(after(turned, gradient), [slot_d[:last]], [0], size, width)
    (partial_d,) = integrate(turned, [slot_d[last:]], [last], size, width, partial_d)
    gradient = add(
        [totals(partial_d)], [slot_d], [sign(offset_d)], [chosen(PLANE - 2)], gradient
    )
    return gradient.reshape(rows, occ_rows, virt)


def solution(mesh):
    if mesh.shape["occ"] % PLANE:
        raise ValueError("incomplete plane")
    in_specs = (P("aux", "occ", None), P("occ"), P(), P("occ", None))
    out_specs = P("aux", "occ", None)
    return jax.shard_map(
        on_device, mesh=mesh, in_specs=in_specs, out_specs=out_specs, check_vma=False
    )
```

time: 150 us -> 237 us (1.58)
  the two profiles are of different devices: /device:TPU:0 before, /device:TPU:13 now
where the time goes in v2:
time: 237 us; the launch traced here: 235 us
  starting transfers between devices  108 us (46%)
  waiting for transfers between devices  44.9 us (19%)
  Pallas kernels  40.4 us (17%)
  local copies, waits for them, and re-layouts  35.2 us (15%)
  between operations  6.61 us (3%)
    ppermute x21, starting transfers between devices, within(): lax.ppermute(block, 'occ', [(g + a, g + b) for g in planes for a, b in mo...  59.5 us
    pallas_call x9, Pallas kernels, call(): pl.pallas_call(kernel, out_shape=outputs, in_specs=specs, out_specs=[pl.B...  40.4 us
    ppermute x8, starting transfers between devices, shifted(): lax.ppermute(block, 'occ', [(g, g + offset) for g in range(groups - offse...  37.8 us
    ppermute x8, waiting for transfers between devices, shifted(): lax.ppermute(block, 'occ', [(g, g + offset) for g in range(groups - offse...  32.8 us
    unnamed x108, local copies, waits for them, and re-layouts  30.8 us
    ppermute x21, waiting for transfers between devices, within(): lax.ppermute(block, 'occ', [(g + a, g + b) for g in planes for a, b in mo...  11.7 us
    ppermute x5, starting transfers between devices, totals(): return [partial, lax.ppermute(partial, 'aux', [(0, 1), (1, 0)])]  10.6 us
  transfers between devices with their start and end apart: 34, of which 8 were waited for; matrix products, arithmetic and copies ran while one was open for 1% of the time, Pallas kernels for 13%

profile of v2, /device:TPU:13, one launch (start us, length us, event | category | flops | bytes accessed | tf_op | source)
XLA Modules:
  0.0 235.1 jit_solution(4316247907128079977)
XLA Ops:
  1.6 3.2 %collective-permute-start.2 = (f32[1024,128]{1,0:T(8,128)S(1)}, f32[1024,128]{1,0:T(8,128)S(1)}, u32[]{:S(2)}, u32[]{:S(2)}) collective-permute-start(f32[1024,128]{1,0:T(8,128)S(1)} %bitcast.26), channel_id=1, source_target_pairs={{0,4},{1,5},{2,6},{3,7},{4,8},{5,9},{6,10},{7,11},{8,12},{9,13},{1... | collective-permute-start | bytes 1572872 | tf_op jit(solution)/shard_map/ppermute | solution.py:186
  6.7 4.1 %collective-permute-start.8 = (f32[2048,128]{1,0:T(8,128)S(1)}, f32[2048,128]{1,0:T(8,128)}, u32[]{:S(2)}, u32[]{:S(2)}) collective-permute-start(f32[2048,128]{1,0:T(8,128)S(1)} %bitcast.23), channel_id=1, source_target_pairs={{0,1},{2,3},{4,5},{6,7},{8,9},{10,11},{12,13},{14,15},{16,17},{18,... | collective-permute-start | bytes 3145736 | tf_op jit(solution)/shard_map/ppermute | solution.py:190
  13.4 6.0 %collective-permute-start = (f32[1]{0:T(128)}, f32[1]{0:T(128)}, u32[]{:S(2)}, u32[]{:S(2)}) collective-permute-start(f32[1]{0:T(128)} %param.5), channel_id=1, source_target_pairs={{0,3},{1,4},{2,5},{3,6},{4,7},{5,8},{6,9},{7,10},{8,11},{9,12},{10... | collective-permute-start | bytes 20 | tf_op jit(solution)/shard_map/ppermute | solution.py:186
  19.5 3.5 %shard_map.46 = (bf16[512,1024]{1,0:T(8,128)(2,1)S(1)}, bf16[512,1024]{1,0:T(8,128)(2,1)S(1)}, f32[512,512]{1,0:T(8,128)}) custom-call(f32[4096,128]{1,0:T(8,128)S(1)} %bitcast.14), custom_call_target="tpu_custom_call" | custom-call | flops 1610612736 | bytes 5242880 | tf_op jit(solution)/shard_map/pallas_call | solution.py:59
  23.0 12.0 %collective-permute-start.1 = (f32[1]{0:T(128)}, f32[1]{0:T(128)}, u32[]{:S(2)}, u32[]{:S(2)}) collective-permute-start(f32[1]{0:T(128)} %param.5), channel_id=1, source_target_pairs={{0,1},{1,2},{2,3},{3,4},{4,5},{5,6},{6,7},{7,8},{8,9},{9,10},{10,1... | collective-permute-start | bytes 20 | tf_op jit(solution)/shard_map/ppermute | solution.py:186
  37.1 3.7 %collective-permute-start.3 = (f32[1]{0:T(128)}, f32[1]{0:T(128)}, u32[]{:S(2)}, u32[]{:S(2)}) collective-permute-start(f32[1]{0:T(128)} %param.5), channel_id=1, source_target_pairs={{0,2},{1,3},{2,4},{3,5},{4,6},{5,7},{6,8},{7,9},{8,10},{9,11},{10,... | collective-permute-start | bytes 20 | tf_op jit(solution)/shard_map/ppermute | solution.py:186
  40.8 20.3 %collective-permute-done.3.refs_2_ = f32[1]{0:T(128)} collective-permute-done((f32[1]{0:T(128)}, f32[1]{0:T(128)}, u32[]{:S(2)}, u32[]{:S(2)}) %collective-permute-start.3) | collective-permute-done | bytes 36 | tf_op jit(solution)/shard_map/ppermute | solution.py:186
  70.3 9.1 %collective-permute-done.5.refs_1_.refs_10_ = f32[1024,128]{1,0:T(8,128)S(1)} collective-permute-done((f32[1024,128]{1,0:T(8,128)S(1)}, f32[1024,128]{1,0:T(8,128)S(1)}, u32[]{:S(2)}, u32[]{:S(2)}) %collective-permute-start.5) | collective-permute-done | bytes 524320 | tf_op jit(solution)/shard_map/ppermute | solution.py:186
  80.8 3.2 %collective-permute-start.12 = (f32[1024,128]{1,0:T(8,128)S(1)}, f32[1024,128]{1,0:T(8,128)}, u32[]{:S(2)}, u32[]{:S(2)}) collective-permute-start(f32[1024,128]{1,0:T(8,128)S(1)} %slice.35), channel_id=1, source_target_pairs={{0,4},{1,5},{2,6},{3,7},{4,8},{5,9},{6,10},{7,11},{8,12},{9,13},{1... | collective-permute-start | bytes 1572872 | tf_op jit(solution)/shard_map/ppermute | solution.py:186
  87.6 3.3 %collective-permute-start.27 = (f32[2048,128]{1,0:T(8,128)S(1)}, f32[2048,128]{1,0:T(8,128)S(1)}, u32[]{:S(2)}, u32[]{:S(2)}) collective-permute-start(f32[2048,128]{1,0:T(8,128)S(1)} %slice.34), channel_id=1, source_target_pairs={{0,1},{2,3},{4,5},{6,7},{8,9},{10,11},{12,13},{14,15},{16,17},{18,... | collective-permute-start | bytes 3145736 | tf_op jit(solution)/shard_map/ppermute | solution.py:190
  95.0 6.1 %collective-permute-start.23 = (f32[1024,128]{1,0:T(8,128)}, f32[1024,128]{1,0:T(8,128)S(1)}, u32[]{:S(2)}, u32[]{:S(2)}) collective-permute-start(f32[1024,128]{1,0:T(8,128)} %collective-permute-done.12.refs_2_.refs_11_), channel_id=1, source_target_pairs={{6,4},{7,5},{10,8},{11,9},{14,12},{15,13},{22,20},{23,21},{26,24},... | collective-permute-start | bytes 1572872 | tf_op jit(solution)/shard_map/ppermute | solution.py:190
  101.2 3.7 %collective-permute-done.29.refs_2_.refs_10_ = f32[1024,128]{1,0:T(8,128)S(1)} collective-permute-done((f32[1024,128]{1,0:T(8,128)S(1)}, f32[1024,128]{1,0:T(8,128)S(1)}, u32[]{:S(2)}, u32[]{:S(2)}) %collective-permute-start.29) | collective-permute-done | bytes 524320 | tf_op jit(solution)/shard_map/ppermute | solution.py:190
  109.7 4.6 %collective-permute-start.28 = (f32[512,512]{1,0:T(8,128)}, f32[512,512]{1,0:T(8,128)}, u32[]{:S(2)}, u32[]{:S(2)}) collective-permute-start(f32[512,512]{1,0:T(8,128)} %get-tuple-element.37.refs_4_), channel_id=1, source_target_pairs={{0,16},{16,0},{1,17},{17,1},{2,18},{18,2},{3,19},{19,3},{4,20},{20... | collective-permute-start | bytes 3145736 | tf_op jit(solution)/shard_map/ppermute | solution.py:194
  117.7 4.1 %shard_map.47.refs_6_ = f32[512,512]{1,0:T(8,128)} custom-call(bf16[512,1024]{1,0:T(8,128)(2,1)S(1)} %get-tuple-element.47.high_ref, bf16[512,1024]{1,0:T(8,128)(2,1)S(1)} %get-tuple-element.48.low_ref, f32[1024,128]{1,0:T(8,128)S(1)} %collective-permute-done.2.refs_0_.refs_9_, f32[1024,128]{1,0:T(8,128)S(1)} %collective-permute-done.5.refs_1_.refs_10_, ...), custom_call_target="tpu_custom_call" | custom-call | flops 1610612736 | bytes 5242880 | tf_op jit(solution)/shard_map/pallas_call | solution.py:59
  121.8 4.2 %collective-permute-start.30 = (f32[512,512]{1,0:T(8,128)}, f32[512,512]{1,0:T(8,128)}, u32[]{:S(2)}, u32[]{:S(2)}) collective-permute-start(f32[512,512]{1,0:T(8,128)} %shard_map.47.refs_6_), channel_id=1, source_target_pairs={{0,16},{16,0},{1,17},{17,1},{2,18},{18,2},{3,19},{19,3},{4,20},{20... | collective-permute-start | bytes 3145736 | tf_op jit(solution)/shard_map/ppermute | solution.py:194
  128.1 4.8 %collective-permute-start.11 = (f32[2048,128]{1,0:T(8,128)S(1)}, f32[2048,128]{1,0:T(8,128)}, u32[]{:S(2)}, u32[]{:S(2)}) collective-permute-start(f32[2048,128]{1,0:T(8,128)S(1)} %collective-permute-done.10.refs_8_.refs_2_.refs_17_), channel_id=1, source_target_pairs={{2,3},{3,2},{6,7},{7,6},{10,11},{11,10},{14,15},{15,14},{18,19},{1... | collective-permute-start | bytes 3145736 | tf_op jit(solution)/shard_map/ppermute | solution.py:190
  135.1 6.7 %collective-permute-done.25.refs_4_.refs_12_ = f32[1024,128]{1,0:T(8,128)} collective-permute-done((f32[1024,128]{1,0:T(8,128)}, f32[1024,128]{1,0:T(8,128)}, u32[]{:S(2)}, u32[]{:S(2)}) %collective-permute-start.25) | collective-permute-done | bytes 524320 | tf_op jit(solution)/shard_map/ppermute | solution.py:190
  141.8 17.1 %collective-permute-start.26 = (f32[1024,128]{1,0:T(8,128)}, f32[1024,128]{1,0:T(8,128)}, u32[]{:S(2)}, u32[]{:S(2)}) collective-permute-start(f32[1024,128]{1,0:T(8,128)} %collective-permute-done.25.refs_4_.refs_12_), channel_id=1, source_target_pairs={{6,4},{10,8},{14,12},{22,20},{26,24},{30,28}} | collective-permute-start | bytes 1572872 | tf_op jit(solution)/shard_map/ppermute | solution.py:190
  167.9 7.5 %shard_map.48.refs_20_ = f32[4096,128]{1,0:T(8,128)S(1)} custom-call(f32[2]{0:T(128)S(1)} %pad_maximum_fusion.1.sign_ref, f32[1]{0:T(128)S(6)} %copy.6.refs_0_.refs_1_, f32[1]{0:T(128)S(6)} %copy.6.refs_0_.refs_1_, f32[1]{0:T(128)} %collective-permute-done.4.refs_2_, f32[1,512]{1,0:T(1,128)S(1)} %bitcast.20, f32[512,512]{1,0:T(8,128)} %get-tuple-element.37.refs_4_, ...), custom_call_target="tpu_custom_call" | custom-call | flops 3221225472 | bytes 10487808 | tf_op jit(solution)/shard_map/pallas_call | solution.py:59
  176.8 4.0 %shard_map.49 = (f32[512,512]{1,0:T(8,128)S(1)}, f32[512,512]{1,0:T(8,128)S(1)}) custom-call(bf16[512,1024]{1,0:T(8,128)(2,1)S(1)} %get-tuple-element.47.high_ref, bf16[512,1024]{1,0:T(8,128)(2,1)S(1)} %get-tuple-element.48.low_ref, f32[2048,128]{1,0:T(8,128)} %collective-permute-done.8.refs_0_.refs_8_, f32[1024,128]{1,0:T(8,128)S(1)} %copy-done.26, ...), custom_call_target="tpu_custom_call" | custom-call | flops 2415919104 | bytes 11534336 | tf_op jit(solution)/shard_map/pallas_call | solution.py:59
  185.8 4.9 %collective-permute-start.19 = (f32[1024,128]{1,0:T(8,128)}, f32[1024,128]{1,0:T(8,128)S(1)}, u32[]{:S(2)}, u32[]{:S(2)}) collective-permute-start(f32[1024,128]{1,0:T(8,128)} %copy-done.15), channel_id=1, source_target_pairs={{6,4},{10,8},{14,12},{22,20},{26,24},{30,28}} | collective-permute-start | bytes 1572872 | tf_op jit(solution)/shard_map/ppermute | solution.py:190
  203.4 7.4 %shard_map.51.refs_14_ = f32[4096,128]{1,0:T(8,128)S(1)} custom-call(f32[2]{0:T(128)S(1)} %pad_maximum_fusion.sign_ref, f32[1]{0:T(128)S(6)} %copy.6.refs_0_.refs_1_, f32[1]{0:T(128)S(6)} %select_n.60.refs_1_, f32[1]{0:T(128)} %collective-permute-done.3.refs_2_, f32[1,512]{1,0:T(1,128)S(1)} %bitcast.21, f32[512,512]{1,0:T(8,128)} %get-tuple-element.45.refs_4_, ...), custom_call_target="tpu_custom_call" | custom-call | flops 3221225472 | bytes 16779264 | tf_op jit(solution)/shard_map/pallas_call | solution.py:59
  210.9 4.0 %shard_map.52.refs_3_ = f32[512,512]{1,0:T(8,128)S(1)} custom-call(bf16[512,1024]{1,0:T(8,128)(2,1)S(1)} %get-tuple-element.47.high_ref, bf16[512,1024]{1,0:T(8,128)(2,1)S(1)} %get-tuple-element.48.low_ref, f32[2048,128]{1,0:T(8,128)S(1)} %copy-done.11, f32[2048,128]{1,0:T(8,128)} %collective-permute-done.20.refs_1_.refs_6_, f32[1024,128]{1,0:T(8,128)S(1)} %copy-done.20, ...), custom_call_target="tpu_custom_call" | custom-call | flops 1207959552 | bytes 8388608 | tf_op jit(solution)/shard_map/pallas_call | solution.py:59
  229.5 5.6 %shard_map.54 = f32[4096,128]{1,0:T(8,128)} custom-call(f32[1]{0:T(128)} %bitcast.1.sign_ref, f32[1]{0:T(128)S(6)} %copy.6.refs_0_.refs_1_, f32[1]{0:T(128)S(6)} %select_n.56.refs_1_, f32[1,512]{1,0:T(1,128)S(1)} %bitcast.22, f32[512,512]{1,0:T(8,128)S(1)} %shard_map.53.refs_3_, f32[512,512]{1,0:T(8,128)S(1)} %copy-done.45, f32[2048,128]{1,0:T(8,128)S(1)} %copy-done.12, ...), custom_call_target="tpu_custom_call" | custom-call | flops 1610612736 | bytes 12584960 | tf_op jit(solution)/shard_map/pallas_call | solution.py:59
  (170 shorter events, 75.3 us)
Async XLA Ops:
  1.6 64.2 %collective-permute-start.2 = (f32[1024,128]{1,0:T(8,128)S(1)}, f32[1024,128]{1,0:T(8,128)S(1)}, u32[]{:S(2)}, u32[]{:S(2)}) collective-permute-start(f32[1024,128]{1,0:T(8,128)S(1)} %bitcast.26), channel_id=1, source_target_pairs={{0,4},{1,5},{2,6},{3,7},{4,8},{5,9},{6,10},{7,11},{8,12},{9,13},{1... | collective-permute-start | bytes 1572872 | tf_op jit(solution)/shard_map/ppermute | solution.py:186
  6.7 74.0 %collective-permute-start.8 = (f32[2048,128]{1,0:T(8,128)S(1)}, f32[2048,128]{1,0:T(8,128)}, u32[]{:S(2)}, u32[]{:S(2)}) collective-permute-start(f32[2048,128]{1,0:T(8,128)S(1)} %bitcast.23), channel_id=1, source_target_pairs={{0,1},{2,3},{4,5},{6,7},{8,9},{10,11},{12,13},{14,15},{16,17},{18,... | collective-permute-start | bytes 3145736 | tf_op jit(solution)/shard_map/ppermute | solution.py:190
  10.8 69.9 %collective-permute-start.7 = (f32[2048,128]{1,0:T(8,128)S(1)}, f32[2048,128]{1,0:T(8,128)S(1)}, u32[]{:S(2)}, u32[]{:S(2)}) collective-permute-start(f32[2048,128]{1,0:T(8,128)S(1)} %bitcast.24), channel_id=1, source_target_pairs={{1,2},{5,6},{9,10},{13,14},{17,18},{21,22},{25,26},{29,30}} | collective-permute-start | bytes 3145736 | tf_op jit(solution)/shard_map/ppermute | solution.py:190
  12.1 68.6 %collective-permute-start.9 = (f32[2048,128]{1,0:T(8,128)S(1)}, f32[2048,128]{1,0:T(8,128)S(1)}, u32[]{:S(2)}, u32[]{:S(2)}) collective-permute-start(f32[2048,128]{1,0:T(8,128)S(1)} %bitcast.25), channel_id=1, source_target_pairs={{0,2},{1,3},{4,6},{5,7},{8,10},{9,11},{12,14},{13,15},{16,18},{17,... | collective-permute-start | bytes 3145736 | tf_op jit(solution)/shard_map/ppermute | solution.py:190
  23.0 14.1 %collective-permute-start.1 = (f32[1]{0:T(128)}, f32[1]{0:T(128)}, u32[]{:S(2)}, u32[]{:S(2)}) collective-permute-start(f32[1]{0:T(128)} %param.5), channel_id=1, source_target_pairs={{0,1},{1,2},{2,3},{3,4},{4,5},{5,6},{6,7},{7,8},{8,9},{9,10},{10,1... | collective-permute-start | bytes 20 | tf_op jit(solution)/shard_map/ppermute | solution.py:186
  37.1 24.1 %collective-permute-start.3 = (f32[1]{0:T(128)}, f32[1]{0:T(128)}, u32[]{:S(2)}, u32[]{:S(2)}) collective-permute-start(f32[1]{0:T(128)} %param.5), channel_id=1, source_target_pairs={{0,2},{1,3},{2,4},{3,5},{4,6},{5,7},{6,8},{7,9},{8,10},{9,11},{10,... | collective-permute-start | bytes 20 | tf_op jit(solution)/shard_map/ppermute | solution.py:186
  65.7 13.6 %collective-permute-start.5 = (f32[1024,128]{1,0:T(8,128)S(1)}, f32[1024,128]{1,0:T(8,128)S(1)}, u32[]{:S(2)}, u32[]{:S(2)}) collective-permute-start(f32[1024,128]{1,0:T(8,128)S(1)} %slice.31), channel_id=1, source_target_pairs={{0,4},{1,5},{2,6},{3,7},{4,8},{5,9},{6,10},{7,11},{8,12},{9,13},{1... | collective-permute-start | bytes 1572872 | tf_op jit(solution)/shard_map/ppermute | solution.py:186
  80.8 13.5 %collective-permute-start.12 = (f32[1024,128]{1,0:T(8,128)S(1)}, f32[1024,128]{1,0:T(8,128)}, u32[]{:S(2)}, u32[]{:S(2)}) collective-permute-start(f32[1024,128]{1,0:T(8,128)S(1)} %slice.35), channel_id=1, source_target_pairs={{0,4},{1,5},{2,6},{3,7},{4,8},{5,9},{6,10},{7,11},{8,12},{9,13},{1... | collective-permute-start | bytes 1572872 | tf_op jit(solution)/shard_map/ppermute | solution.py:186
  86.3 28.8 %collective-permute-start.10 = (f32[2048,128]{1,0:T(8,128)S(1)}, f32[2048,128]{1,0:T(8,128)S(1)}, u32[]{:S(2)}, u32[]{:S(2)}) collective-permute-start(f32[2048,128]{1,0:T(8,128)S(1)} %slice.34), channel_id=1, source_target_pairs={{0,2},{1,3},{4,6},{5,7},{8,10},{9,11},{12,14},{13,15},{16,18},{17,... | collective-permute-start | bytes 3145736 | tf_op jit(solution)/shard_map/ppermute | solution.py:190
  87.6 29.1 %collective-permute-start.27 = (f32[2048,128]{1,0:T(8,128)S(1)}, f32[2048,128]{1,0:T(8,128)S(1)}, u32[]{:S(2)}, u32[]{:S(2)}) collective-permute-start(f32[2048,128]{1,0:T(8,128)S(1)} %slice.34), channel_id=1, source_target_pairs={{0,1},{2,3},{4,5},{6,7},{8,9},{10,11},{12,13},{14,15},{16,17},{18,... | collective-permute-start | bytes 3145736 | tf_op jit(solution)/shard_map/ppermute | solution.py:190
  94.3 14.6 %collective-permute-start.21 = (f32[1024,128]{1,0:T(8,128)S(1)}, f32[1024,128]{1,0:T(8,128)S(1)}, u32[]{:S(2)}, u32[]{:S(2)}) collective-permute-start(f32[1024,128]{1,0:T(8,128)S(1)} %collective-permute-done.6.refs_6_.refs_15_), channel_id=1, source_target_pairs={{4,5},{5,4},{8,9},{9,8},{12,13},{13,12},{20,21},{21,20},{24,25},{2... | collective-permute-start | bytes 1572872 | tf_op jit(solution)/shard_map/ppermute | solution.py:190
  95.0 19.3 %collective-permute-start.23 = (f32[1024,128]{1,0:T(8,128)}, f32[1024,128]{1,0:T(8,128)S(1)}, u32[]{:S(2)}, u32[]{:S(2)}) collective-permute-start(f32[1024,128]{1,0:T(8,128)} %collective-permute-done.12.refs_2_.refs_11_), channel_id=1, source_target_pairs={{6,4},{7,5},{10,8},{11,9},{14,12},{15,13},{22,20},{23,21},{26,24},... | collective-permute-start | bytes 1572872 | tf_op jit(solution)/shard_map/ppermute | solution.py:190
  109.7 23.9 %collective-permute-start.28 = (f32[512,512]{1,0:T(8,128)}, f32[512,512]{1,0:T(8,128)}, u32[]{:S(2)}, u32[]{:S(2)}) collective-permute-start(f32[512,512]{1,0:T(8,128)} %get-tuple-element.37.refs_4_), channel_id=1, source_target_pairs={{0,16},{16,0},{1,17},{17,1},{2,18},{18,2},{3,19},{19,3},{4,20},{20... | collective-permute-start | bytes 3145736 | tf_op jit(solution)/shard_map/ppermute | solution.py:194
  114.3 13.0 %collective-permute-start.22 = (f32[1024,128]{1,0:T(8,128)S(1)}, f32[1024,128]{1,0:T(8,128)S(1)}, u32[]{:S(2)}, u32[]{:S(2)}) collective-permute-start(f32[1024,128]{1,0:T(8,128)S(1)} %collective-permute-done.13.refs_7_.refs_16_), channel_id=1, source_target_pairs={{4,5},{5,4},{8,9},{9,8},{12,13},{13,12},{20,21},{21,20},{24,25},{2... | collective-permute-start | bytes 1572872 | tf_op jit(solution)/shard_map/ppermute | solution.py:190
  115.0 45.3 %collective-permute-start.20 = (f32[2048,128]{1,0:T(8,128)}, f32[2048,128]{1,0:T(8,128)}, u32[]{:S(2)}, u32[]{:S(2)}) collective-permute-start(f32[2048,128]{1,0:T(8,128)} %collective-permute-done.8.refs_0_.refs_8_), channel_id=1, source_target_pairs={{1,3},{5,7},{9,11},{13,15},{17,19},{21,23},{25,27},{29,31}} | collective-permute-start | bytes 3145736 | tf_op jit(solution)/shard_map/ppermute | solution.py:190
  121.8 39.8 %collective-permute-start.30 = (f32[512,512]{1,0:T(8,128)}, f32[512,512]{1,0:T(8,128)}, u32[]{:S(2)}, u32[]{:S(2)}) collective-permute-start(f32[512,512]{1,0:T(8,128)} %shard_map.47.refs_6_), channel_id=1, source_target_pairs={{0,16},{16,0},{1,17},{17,1},{2,18},{18,2},{3,19},{19,3},{4,20},{20... | collective-permute-start | bytes 3145736 | tf_op jit(solution)/shard_map/ppermute | solution.py:194
  126.0 15.7 %collective-permute-start.25 = (f32[1024,128]{1,0:T(8,128)}, f32[1024,128]{1,0:T(8,128)}, u32[]{:S(2)}, u32[]{:S(2)}) collective-permute-start(f32[1024,128]{1,0:T(8,128)} %collective-permute-done.12.refs_2_.refs_11_), channel_id=1, source_target_pairs={{5,4},{7,6},{9,8},{11,10},{13,12},{15,14},{21,20},{23,22},{25,24},... | collective-permute-start | bytes 1572872 | tf_op jit(solution)/shard_map/ppermute | solution.py:190
  128.1 48.5 %collective-permute-start.11 = (f32[2048,128]{1,0:T(8,128)S(1)}, f32[2048,128]{1,0:T(8,128)}, u32[]{:S(2)}, u32[]{:S(2)}) collective-permute-start(f32[2048,128]{1,0:T(8,128)S(1)} %collective-permute-done.10.refs_8_.refs_2_.refs_17_), channel_id=1, source_target_pairs={{2,3},{3,2},{6,7},{7,6},{10,11},{11,10},{14,15},{15,14},{18,19},{1... | collective-permute-start | bytes 3145736 | tf_op jit(solution)/shard_map/ppermute | solution.py:190
  133.6 43.1 %collective-permute-start.24 = (f32[1024,128]{1,0:T(8,128)}, f32[1024,128]{1,0:T(8,128)}, u32[]{:S(2)}, u32[]{:S(2)}) collective-permute-start(f32[1024,128]{1,0:T(8,128)} %copy-done.37), channel_id=1, source_target_pairs={{4,5},{8,9},{12,13},{20,21},{24,25},{28,29}} | collective-permute-start | bytes 1572872 | tf_op jit(solution)/shard_map/ppermute | solution.py:190
  141.8 34.9 %collective-permute-start.26 = (f32[1024,128]{1,0:T(8,128)}, f32[1024,128]{1,0:T(8,128)}, u32[]{:S(2)}, u32[]{:S(2)}) collective-permute-start(f32[1024,128]{1,0:T(8,128)} %collective-permute-done.25.refs_4_.refs_12_), channel_id=1, source_target_pairs={{6,4},{10,8},{14,12},{22,20},{26,24},{30,28}} | collective-permute-start | bytes 1572872 | tf_op jit(solution)/shard_map/ppermute | solution.py:190
  160.3 20.5 %collective-permute-start.16 = (f32[1024,128]{1,0:T(8,128)}, f32[1024,128]{1,0:T(8,128)S(1)}, u32[]{:S(2)}, u32[]{:S(2)}) collective-permute-start(f32[1024,128]{1,0:T(8,128)} %copy-done.51), channel_id=1, source_target_pairs={{6,4},{7,5},{10,8},{11,9},{14,12},{15,13},{22,20},{23,21},{26,24},... | collective-permute-start | bytes 1572872 | tf_op jit(solution)/shard_map/ppermute | solution.py:190
  161.6 19.1 %collective-permute-start.18 = (f32[1024,128]{1,0:T(8,128)}, f32[1024,128]{1,0:T(8,128)S(1)}, u32[]{:S(2)}, u32[]{:S(2)}) collective-permute-start(f32[1024,128]{1,0:T(8,128)} %copy-done.51), channel_id=1, source_target_pairs={{5,4},{7,6},{9,8},{11,10},{13,12},{15,14},{21,20},{23,22},{25,24},... | collective-permute-start | bytes 1572872 | tf_op jit(solution)/shard_map/ppermute | solution.py:190
  185.1 29.8 %collective-permute-start.17 = (f32[1024,128]{1,0:T(8,128)}, f32[1024,128]{1,0:T(8,128)S(1)}, u32[]{:S(2)}, u32[]{:S(2)}) collective-permute-start(f32[1024,128]{1,0:T(8,128)} %copy-done.13), channel_id=1, source_target_pairs={{4,5},{8,9},{12,13},{20,21},{24,25},{28,29}} | collective-permute-start | bytes 1572872 | tf_op jit(solution)/shard_map/ppermute | solution.py:190
  185.8 29.1 %collective-permute-start.19 = (f32[1024,128]{1,0:T(8,128)}, f32[1024,128]{1,0:T(8,128)S(1)}, u32[]{:S(2)}, u32[]{:S(2)}) collective-permute-start(f32[1024,128]{1,0:T(8,128)} %copy-done.15), channel_id=1, source_target_pairs={{6,4},{10,8},{14,12},{22,20},{26,24},{30,28}} | collective-permute-start | bytes 1572872 | tf_op jit(solution)/shard_map/ppermute | solution.py:190
  (64 other events, 513.0 us)
